TPU v7x, 128 devices: a whole 4x4x4 slice. The times are simulated.
128 devices in a mesh: ctx: 32 (over z, y_hi, x), fsdp: 4 (over y_lo, core).
Axes of the slice: x: 4, y: 4 (y_hi: 2, y_lo: 2; y = y_hi * 2 + y_lo), z: 4, core: 2. Of those that a mesh axis runs over, the one named last changes fastest.
Arguments:
- tokens: bfloat16 [4, 4096, 960], P('fsdp', 'ctx'), may hold values from -6 to 6
- cotangent: bfloat16 [4, 4096, 960], P('fsdp', 'ctx'), may hold values from -6 to 6
- block_table: int32 [64], replicated, may hold values from 0 to 63, as said below
- attn_gain: bfloat16 [960], P('fsdp'), may hold values from 0.5 to 1.5
- w_query: bfloat16 [960, 960], P('fsdp'), may hold values from -0.1875 to 0.1875
- w_key: bfloat16 [960, 320], P('fsdp'), may hold values from -0.1875 to 0.1875
- w_value: bfloat16 [960, 320], P('fsdp'), may hold values from -0.1875 to 0.1875
- w_out: bfloat16 [960, 960], P('fsdp'), may hold values from -1 to 1
- mlp_gain: bfloat16 [960], P('fsdp'), may hold values from 0.5 to 1.5
- w_gate: bfloat16 [960, 2560], P('fsdp'), may hold values from -0.1875 to 0.1875
- w_up: bfloat16 [960, 2560], P('fsdp'), may hold values from -0.1875 to 0.1875
- w_down: bfloat16 [2560, 960], P('fsdp'), may hold values from -0.125 to 0.125
Outputs:
- layer_out: bfloat16 [4, 4096, 960], P('fsdp', 'ctx')
- grad_tokens: float32 [4, 4096, 960], P('fsdp', 'ctx')
- grad_attn_gain: float32 [960], P('fsdp')
- grad_query: float32 [960, 960], P('fsdp')
- grad_key: float32 [960, 320], P('fsdp')
- grad_value: float32 [960, 320], P('fsdp')
- grad_out: float32 [960, 960], P('fsdp')
- grad_mlp_gain: float32 [960], P('fsdp')
- grad_gate: float32 [960, 2560], P('fsdp')
- grad_up: float32 [960, 2560], P('fsdp')
- grad_down: float32 [2560, 960], P('fsdp')
Inputs may be any that keep to these rules, and one draw needn't show every extreme that they name: `block_table`: entries 2c and 2c + 1 are the numbers of the two blocks of 64 positions held by index c of ctx, in the order of its rows; every block number appears once, and the two numbers of one index sum to 63.
All inputs are finite; a program needn't handle non-finite values.
Results may differ from a plain program's by a relative error of at most 0.034.
Values may be sent and summed in bfloat16 or wider, within the bound.
A program may use at most 192 MiB of HBM per device.

v0:
```python
import functools
import math

import jax
import jax.numpy as jnp
from jax import lax
from jax.experimental import pallas as pl
from jax.experimental.pallas import tpu as pltpu
from jax.sharding import PartitionSpec as P

D = 960
HEADS = 15
KV_HEADS = 5
GROUP = 3
HEAD = 64
FF = 2560
TOK = 128
HALF = 64
CTX = 32
TILES = 33
KEYS = TILES * 128
SCALE = HEAD ** (-0.5)
EPSILON = 1e-05
BASE = 10000.0
LOG2E = math.log2(math.e)
NEG = -1e30
MESH = pl.DeviceIdType.MESH
ANY = pl.BlockSpec(memory_space=pl.ANY)
VM = pl.BlockSpec(memory_space=pltpu.VMEM)
BIG = 56 * 2**20
F32 = jnp.float32
BF16 = jnp.bfloat16


def here():
    ctx = lax.axis_index("ctx")
    shard = lax.axis_index("fsdp")
    return {
        "z": ctx // 8,
        "yh": (ctx // 4) % 2,
        "x": ctx % 4,
        "yl": shard // 2,
        "c": shard % 2,
    }


def device(place, **moved):
    p = {**place, **moved}
    return (p["z"] * 8 + p["yh"] * 4 + p["x"], p["yl"] * 2 + p["c"])


def greet(devices):
    sem = pltpu.get_barrier_semaphore()
    for d in devices:
        pl.semaphore_signal(sem, inc=1, device_id=d, device_id_type=MESH)
    pl.semaphore_wait(sem, len(devices))


class Sems:
    def __init__(self, send, recv):
        self.send, self.recv, self.at = send, recv, 0

    def push(self, src, dst, dev):
        copy = pltpu.make_async_remote_copy(
            src_ref=src,
            dst_ref=dst,
            send_sem=self.send.at[self.at],
            recv_sem=self.recv.at[self.at],
            device_id=dev,
            device_id_type=MESH,
        )
        self.at += 1
        copy.start()
        return copy


def start_gather(me, sems, local, arrays):
    f = me["yl"] * 2 + me["c"]
    near = device(me, yl=1 - me["yl"])
    far = device(me, yl=1 - me["yl"], yh=1 - me["yh"])
    mate = device(me, c=1 - me["c"])
    parts, kept, own = [], [], []
    for i, (a, b) in enumerate(arrays):
        rows = a.shape[0]
        first = rows // 32 * 16 if i % 2 else (rows + 31) // 32 * 16
        for lo, size, dev in ((0, first, near), (first, rows - first, far)):
            if size:
                src = a.at[pl.ds(lo, size)]
                dst = b.at[pl.ds(pl.multiple_of(f * rows + lo, 16), size)]
                parts.append((sems.push(src, dst, dev), b, rows, lo, size))
    for i, (a, b) in enumerate(arrays):
        rows = a.shape[0]
        dst = b.at[pl.ds(pl.multiple_of(f * rows, 16), rows)]
        kept.append(sems.push(a, dst, mate))
        copy = pltpu.make_async_copy(a, dst, local.at[i])
        copy.start()
        own.append(copy)
    return parts, kept, own


def relay_gather(me, sems, started):
    parts, kept, _ = started
    across = (1 - me["yl"]) * 2 + me["c"]
    mate = device(me, c=1 - me["c"])
    for copy, b, rows, lo, size in parts:
        copy.wait_recv()
        span = b.at[pl.ds(pl.multiple_of(across * rows + lo, 16), size)]
        kept.append(sems.push(span, span, mate))


def end_gather(started):
    parts, kept, own = started
    for copy in own:
        copy.wait()
    for copy in kept:
        copy.wait()
    for copy, *_ in parts:
        copy.wait_send()


def gather_kernel(count, *refs):
    arrays = list(zip(refs[:count], refs[count : 2 * count]))
    send, recv, local = refs[2 * count :]
    me = here()
    flip = 1 - me["yl"]
    greet((device(me, yl=flip), device(me, yl=flip, yh=1 - me["yh"]), device(me, c=1 - me["c"])))
    sems = Sems(send, recv)
    started = start_gather(me, sems, local, arrays)
    relay_gather(me, sems, started)
    end_gather(started)


def gathered(arrays):
    return [jax.ShapeDtypeStruct((4 * a.shape[0], *a.shape[1:]), a.dtype) for a in arrays]


def gather_weights(arrays, collective_id):
    n = len(arrays)
    return pl.pallas_call(
        functools.partial(gather_kernel, n),
        out_shape=gathered(arrays),
        in_specs=[VM] * n,
        out_specs=[ANY] * n,
        scratch_shapes=[
            pltpu.SemaphoreType.DMA((5 * n,)),
            pltpu.SemaphoreType.DMA((5 * n,)),
            pltpu.SemaphoreType.DMA((n,)),
        ],
        compiler_params=pltpu.CompilerParams(
            collective_id=collective_id, has_side_effects=True, vmem_limit_bytes=BIG
        ),
        name="gather_weights",
    )(*arrays)


def around(me, axis):
    return [(d, lax.rem(me[axis] + d, 4)) for d in (1, 3, 2)]


def gather_kv(me, sems, kv, out, once_across):
    x, yh, z = me["x"], me["yh"], me["z"]
    other = device(me, yh=1 - yh)
    xs = [device(me, x=at) for _, at in around(me, "x")]
    zs = [device(me, z=at) for _, at in around(me, "z")]
    key, value = pl.ds(0, 320), pl.ds(320, 320)
    step1 = [sems.push(kv.at[p], out.at[z, yh, x, p], other) for p in (key, value)]
    step2 = {}
    step2[0, 0] = [sems.push(kv.at[key], out.at[z, yh, x, key], dev) for dev in xs]
    step2[1, 0] = [sems.push(kv.at[value], out.at[z, yh, x, value], dev) for dev in zs]
    out[z, yh, x] = kv[...]
    step3 = []
    for hop in (0, 1):
        row = yh if hop == 0 else 1 - yh
        for axis, (devs, p) in enumerate(((zs, key), (xs, value))):
            for c in step2[axis, hop]:
                c.wait_recv()
            span = out.at[z, row, :, key] if axis == 0 else out.at[:, row, x, value]
            for dev in devs:
                step3.append(sems.push(span, span, dev))
        if hop == 0:
            for axis, (devs, p) in enumerate(((xs, key), (zs, value))):
                step1[axis].wait_recv()
                span = out.at[z, 1 - yh, x, p]
                step2[axis, 1] = [sems.push(span, span, dev) for dev in devs]
            once_across()
    for c in step3:
        c.wait_recv()
    return step1 + sum(step2.values(), []) + step3


class Scatter:
    COPIES = 26
    SCRATCH = [
        pltpu.VMEM((3, 2, 4, 320, 128), BF16),
        pltpu.VMEM((3, 2, 4, 320, 128), BF16),
        pltpu.VMEM((2, 4, 320, 128), BF16),
        pltpu.VMEM((2, 4, 320, 128), BF16),
        pltpu.VMEM((3, 2, 320, 128), BF16),
        pltpu.VMEM((3, 2, 320, 128), BF16),
        pltpu.VMEM((2, 320, 128), BF16),
        pltpu.VMEM((2, 320, 128), BF16),
    ]

    def __init__(self, me, sems, part, out, scratch):
        self.me, self.sems, self.part, self.out = me, sems, part, out
        r1a, r1b, s1a, s1b, r2a, r2b, self.s2, self.r3 = scratch
        self.r1, self.s1, self.r2 = (r1a, r1b), (s1a, s1b), (r2a, r2b)
        self.xs = [(d, at, device(me, x=at)) for d, at in around(me, "x")]
        self.zs = [(d, at, device(me, z=at)) for d, at in around(me, "z")]
        self.rows = (1 - me["yh"], me["yh"])
        self.first, self.second, self.third = {}, {}, []

    def start(self):
        x, z, part, push = self.me["x"], self.me["z"], self.part, self.sems.push
        key, value = pl.ds(0, 320), pl.ds(320, 320)
        for r, row in enumerate(self.rows):
            for d, at, dev in self.zs:
                src = part.at[at, row, :, key]
                self.first[0, r, d] = push(src, self.r1[0].at[d - 1, r], dev)
            for d, at, dev in self.xs:
                src = part.at[:, row, at, value]
                self.first[1, r, d] = push(src, self.r1[1].at[d - 1, r], dev)

    def middle(self, r):
        x, z, part, row = self.me["x"], self.me["z"], self.part, self.rows[r]
        for axis in (0, 1):
            r1, s1, r2 = self.r1[axis], self.s1[axis], self.r2[axis]
            for d in (1, 2, 3):
                self.first[axis, r, d].wait_recv()
            for i in range(4):
                own = part[z, row, i, 0:320] if axis == 0 else part[i, row, x, 320:640]
                total = own.astype(F32)
                for d in (0, 1, 2):
                    total = total + r1[d, r, i].astype(F32)
                s1[r, i] = total.astype(BF16)
            for d, at, dev in (self.xs, self.zs)[axis]:
                self.second[axis, r, d] = self.sems.push(s1.at[r, at], r2.at[d - 1, r], dev)

    def last(self, r):
        other = device(self.me, yh=1 - self.me["yh"])
        for axis in (0, 1):
            s1, r2 = self.s1[axis], self.r2[axis]
            at = self.me["x"] if axis == 0 else self.me["z"]
            for d in (1, 2, 3):
                self.second[axis, r, d].wait_recv()
            total = s1[r, at].astype(F32)
            for d in (0, 1, 2):
                total = total + r2[d, r].astype(F32)
            if r == 0:
                self.s2[axis] = total.astype(BF16)
                self.third.append(self.sems.push(self.s2.at[axis], self.r3.at[axis], other))
            else:
                self.out[pl.ds(axis * 320, 320), :] = total

    def end(self):
        for axis in (0, 1):
            self.third[axis].wait_recv()
            span = pl.ds(axis * 320, 320)
            self.out[span, :] = self.out[span, :] + self.r3[axis].astype(F32)
        for c in list(self.first.values()) + list(self.second.values()) + self.third:
            c.wait_send()


def build_tiles(head, kv_ref, own_ref, left_ref, tiles_ref, base):
    lane = lax.broadcasted_iota(jnp.int32, (HALF, 128), 1)
    start = pl.multiple_of(base + head * HALF, HALF)

    def one(i, _):
        block = kv_ref[i, pl.ds(start, HALF), :].astype(F32)
        top = jnp.where(lane < HALF, block, 0.0)
        low = pltpu.roll(block, HALF, 1) * left_ref[pl.ds(i, 1), :]
        at = pl.multiple_of(i * 128, 128)
        tiles_ref[pl.ds(at, 128), :] = jnp.concatenate([top, low], axis=0).astype(BF16)
        return 0

    lax.fori_loop(0, CTX, one, 0, unroll=32)
    block = own_ref[pl.ds(start, HALF), :].astype(F32)
    top = jnp.where(lane < HALF, 0.0, pltpu.roll(block, HALF, 1))
    tiles_ref[pl.ds(CTX * 128, 128), :] = jnp.concatenate(
        [top, jnp.zeros_like(top)], axis=0
    ).astype(BF16)


def dot_nt(a, b):
    return lax.dot_general(a, b, (((1,), (1,)), ((), ())), preferred_element_type=F32)


def dot_nn(a, b):
    return lax.dot_general(a, b, (((1,), (0,)), ((), ())), preferred_element_type=F32)


ROWS = GROUP * HALF


def row_offset():
    return lax.rem(lax.broadcasted_iota(jnp.int32, (ROWS, 128), 0), HALF).astype(F32)


def attend_head(head, q, kv_ref, own_ref, flag_ref, left_ref, limit_ref, kk, vv):
    build_tiles(head, kv_ref, own_ref, left_ref, kk, 0)
    build_tiles(head, kv_ref, own_ref, left_ref, vv, 320)
    offset = row_offset()
    low = jnp.full((ROWS, 128), NEG, F32)
    s = dot_nt(q, kk[...]) * (SCALE * LOG2E)
    tiles = []
    top_l, top_e = low, low
    for i in range(TILES):
        tile = s[:, i * 128 : (i + 1) * 128]
        tile = jnp.where(limit_ref[i : i + 1, :] <= offset, tile, NEG)
        tiles.append(tile)
        late = flag_ref[i : i + 1, :] > 0.5
        top_l = jnp.maximum(top_l, jnp.where(late, tile, NEG))
        top_e = jnp.maximum(top_e, jnp.where(late, NEG, tile))
    max_l = jnp.broadcast_to(jnp.max(top_l, axis=1, keepdims=True), (ROWS, 128))
    max_e = jnp.broadcast_to(jnp.max(top_e, axis=1, keepdims=True), (ROWS, 128))
    sum_l = jnp.zeros((ROWS, 128), F32)
    sum_e = jnp.zeros((ROWS, 128), F32)
    probs = []
    for i in range(TILES):
        late = flag_ref[i : i + 1, :] > 0.5
        p = jnp.exp2(tiles[i] - jnp.where(late, max_l, max_e))
        p_l = jnp.where(late, p, 0.0)
        sum_l = sum_l + p_l
        sum_e = sum_e + (p - p_l)
        probs.append(p.astype(BF16))
    total = dot_nn(jnp.concatenate(probs, axis=1), vv[...])
    late = lax.broadcasted_iota(jnp.int32, (ROWS, 128), 1) < HALF
    row_sum = jnp.where(
        late, jnp.sum(sum_l, axis=1, keepdims=True), jnp.sum(sum_e, axis=1, keepdims=True)
    )
    return total / row_sum, jnp.where(late, max_l, max_e) + jnp.log2(row_sum)


def forward_kernel(count, q_ref, own_ref, flag_ref, left_ref, limit_ref, *refs):
    shards, refs = refs[:count], refs[count:]
    o_ref, l_ref, kv_out, *full = refs[: 3 + count]
    kv, kk, vv, send, recv, local = refs[3 + count :]
    me = here()
    greet_axes(me)
    sems = Sems(send, recv)
    started = []

    def start_weights():
        started.extend(start_gather(me, sems, local, list(zip(shards, full))))

    kv_copies = gather_kv(me, sems, own_ref, kv, start_weights)
    keep = pltpu.make_async_copy(kv, kv_out, local.at[count])
    keep.start()
    flat = kv.reshape(CTX, 640, 128)

    def one(head, _):
        o, logs = attend_head(
            head, q_ref[head], flat, own_ref, flag_ref, left_ref, limit_ref, kk, vv
        )
        o_ref[head] = o
        l_ref[head] = logs
        return 0

    lax.fori_loop(0, 3, one, 0)
    relay_gather(me, sems, started)
    lax.fori_loop(3, KV_HEADS, one, 0)
    end_gather(started)
    for copy in kv_copies:
        copy.wait_send()
    keep.wait()


def forward(q, own, plan, shards, collective_id):
    flags, left, _, limits = plan
    n = len(shards)
    copies = 5 * n + 26
    return pl.pallas_call(
        functools.partial(forward_kernel, n),
        out_shape=[jax.ShapeDtypeStruct((KV_HEADS, ROWS, 128), F32)] * 2
        + [jax.ShapeDtypeStruct((4, 2, 4, 640, 128), BF16)]
        + gathered(shards),
        in_specs=[VM] * (5 + n),
        out_specs=[VM, VM, ANY] + [ANY] * n,
        scratch_shapes=[
            pltpu.VMEM((4, 2, 4, 640, 128), BF16),
            pltpu.VMEM((KEYS, 128), BF16),
            pltpu.VMEM((KEYS, 128), BF16),
            pltpu.SemaphoreType.DMA((copies,)),
            pltpu.SemaphoreType.DMA((copies,)),
            pltpu.SemaphoreType.DMA((n + 1,)),
        ],
        compiler_params=pltpu.CompilerParams(
            collective_id=collective_id, has_side_effects=True, vmem_limit_bytes=BIG
        ),
        name="forward",
    )(q, own, flags, left, limits, *shards)


def attend_back_head(
    head, q, do, o, logs, kv_ref, own_ref, flag_ref, left_ref, right_ref, limit_ref,
    dkv_ref, kk, vv,
):
    build_tiles(head, kv_ref, own_ref, left_ref, kk, 0)
    build_tiles(head, kv_ref, own_ref, left_ref, vv, 320)
    offset = row_offset()
    lane = lax.broadcasted_iota(jnp.int32, (ROWS, 128), 1)
    product = do.astype(F32) * o
    shape = (ROWS, 128)
    delta_l = jnp.broadcast_to(
        jnp.sum(jnp.where(lane < HALF, product, 0.0), axis=1, keepdims=True), shape
    )
    delta_e = jnp.broadcast_to(
        jnp.sum(jnp.where(lane < HALF, 0.0, product), axis=1, keepdims=True), shape
    )
    log_l = jnp.broadcast_to(logs[:, 0:1], shape)
    log_e = jnp.broadcast_to(logs[:, HALF : HALF + 1], shape)
    k_rows = pl.ds(pl.multiple_of(head * HALF, HALF), HALF)
    v_rows = pl.ds(pl.multiple_of(320 + head * HALF, HALF), HALF)
    small = lax.broadcasted_iota(jnp.int32, (HALF, 128), 1)
    keys = kk[...]
    s = dot_nt(q, keys) * (SCALE * LOG2E)
    dp = dot_nt(do, vv[...])
    probs, scores = [], []
    for i in range(TILES):
        cut = slice(i * 128, (i + 1) * 128)
        late = flag_ref[i : i + 1, :] > 0.5
        tile = jnp.where(limit_ref[i : i + 1, :] <= offset, s[:, cut], NEG)
        p = jnp.exp2(tile - jnp.where(late, log_l, log_e))
        probs.append(p.astype(BF16))
        scores.append((p * (dp[:, cut] - jnp.where(late, delta_l, delta_e))).astype(BF16))
    ds = jnp.concatenate(scores, axis=1)
    dq = dot_nn(ds, keys) * SCALE
    dk = dot_nn(q.astype(F32).T.astype(BF16), ds) * SCALE
    dv = dot_nn(do.astype(F32).T.astype(BF16), jnp.concatenate(probs, axis=1))
    mine = lax.axis_index("ctx")
    for rows, both in ((k_rows, dk), (v_rows, dv)):
        for i in range(CTX):
            cut = slice(i * 128, (i + 1) * 128)
            top, bottom = both[0:HALF, cut], both[HALF:128, cut]
            total = (
                top * flag_ref[i : i + 1, :]
                + pltpu.roll(bottom, HALF, 1) * right_ref[i : i + 1, :]
            )
            dkv_ref[i, rows, :] = total.astype(BF16)
        bottom = both[HALF:128, CTX * 128 :]
        before = dkv_ref[mine, rows, :].astype(F32)
        dkv_ref[mine, rows, :] = (before + jnp.where(small < HALF, bottom, 0.0)).astype(BF16)
    return dq


def pop(refs, count):
    taken = refs[:count]
    del refs[:count]
    return taken


class Reduction:
    def __init__(self, jobs, extra):
        self.operands, self.jobs, self.scratch, rows = [], [], [], 0
        for left, right in jobs:
            self.operands += [left, right]
            m, n = left.shape[-2], right.shape[-1]
            self.jobs.append((left.ndim == 4, m, right.ndim == 4, n))
            self.scratch.append(pltpu.VMEM((left.shape[0], m, 256), BF16))
            self.scratch.append(pltpu.VMEM((right.shape[0], 256, n), BF16))
            rows += m * (n // 128)
        self.extra = extra is not None
        if self.extra:
            self.operands.append(extra)
            self.scratch.append(pltpu.VMEM((2, 2, 16, 128), BF16))
            rows += 16
        pieces = -(-rows // 256)
        self.sizes = ((pieces + 1) // 2 * 16, pieces // 2 * 16)
        self.used = 16 * sum(self.sizes)
        self.scratch.append(pltpu.VMEM((2, self.used, 128), BF16))
        for size in self.sizes:
            self.scratch += [
                pltpu.VMEM((3, 4, 2, size, 128), BF16),
                pltpu.VMEM((4, 2, size, 128), BF16),
                pltpu.VMEM((3, 2, size, 128), BF16),
                pltpu.VMEM((2, size, 128), BF16),
                pltpu.VMEM((4, size, 128), BF16),
            ]
        self.locals = 2 * len(jobs) + 1
        self.copies = 2 * len(jobs) + 1 + 24 + 6 + 6
        self.fin_shape = (sum(self.sizes), 128)

    def bind(self, me, sems, local, operands, scratch, fin):
        operands, scratch = list(operands), list(scratch)
        self.me, self.sems, self.local, self.fin = me, sems, local, fin
        self.sources, self.buffers = [], []
        core = me["c"]
        for cut_left, _, cut_right, _ in self.jobs:
            left, right = pop(operands, 2)
            lefts = (left.at[:, core], left.at[:, 1 - core]) if cut_left else (left, left)
            rights = (right.at[:, core], right.at[:, 1 - core]) if cut_right else (right, right)
            self.sources.append((*lefts, *rights))
            self.buffers.append(pop(scratch, 2))
        if self.extra:
            self.extra_refs = (operands[0].at[:, core], operands[0].at[:, 1 - core])
            self.extra_buffer = scratch.pop(0)
        self.grads = scratch.pop(0)
        self.parts = [pop(scratch, 5) for _ in self.sizes]
        xs = [(d, at, device(me, x=at)) for d, at in around(me, "x")]
        zs = [(d, at, device(me, z=at)) for d, at in around(me, "z")]
        x, z = me["x"], me["z"]
        self.plans = (
            (0, self.sizes[0], xs, zs, x, z),
            (16 * self.sizes[0], self.sizes[1], zs, xs, z, x),
        )
        self.first, self.second, self.third = {}, {}, {}

    def trade(self):
        mate = device(self.me, c=1 - self.me["c"])
        push = self.sems.push
        self.mine, self.traded = [], []

        def keep(src, dst):
            copy = pltpu.make_async_copy(src, dst, self.local.at[len(self.mine)])
            copy.start()
            self.mine.append(copy)

        here_, there = pl.ds(0, 128), pl.ds(128, 128)
        for (lm, lt, rm, rt), (lb, rb) in zip(self.sources, self.buffers):
            self.traded.append(push(lt, lb.at[:, :, there], mate))
            self.traded.append(push(rt, rb.at[:, there], mate))
            keep(lm, lb.at[:, :, here_])
            keep(rm, rb.at[:, here_])
        if self.extra:
            self.traded.append(push(self.extra_refs[1], self.extra_buffer.at[1], mate))
            keep(self.extra_refs[0], self.extra_buffer.at[0])

    def multiply(self):
        for copy in self.mine:
            copy.wait()
        for copy in self.traded:
            copy.wait_recv()
        base, grads = 0, self.grads
        for (_, m, _, n), (lb, rb) in zip(self.jobs, self.buffers):
            width = 256 if n % 256 == 0 else 128
            for s in range(2):
                left = lb[min(s, lb.shape[0] - 1)]

                def block(i, _, left=left, rb=rb, s=s, m=m, width=width, base=base):
                    at = pl.multiple_of(i * width, 128)
                    right = rb[min(s, rb.shape[0] - 1), :, pl.ds(at, width)]
                    result = dot_nn(left, right).astype(BF16)
                    for w in range(width // 128):
                        to = pl.multiple_of(base + (i * (width // 128) + w) * m, 16)
                        grads[s, pl.ds(to, m), :] = result[:, w * 128 : (w + 1) * 128]
                    return 0

                lax.fori_loop(0, n // width, block, 0)
            base += m * (n // 128)
        if self.extra:
            for s in range(2):
                both = self.extra_buffer[0, s].astype(F32) + self.extra_buffer[1, s].astype(F32)
                grads[s, pl.ds(base, 16), :] = both.astype(BF16)
            base += 16
        if base < self.used:
            for s in range(2):
                grads[s, pl.ds(base, self.used - base), :] = jnp.zeros(
                    (self.used - base, 128), BF16
                )
        for k in (1, 3, 2, 0):
            for n, (lo, size, ring, _, _, j_me) in enumerate(self.plans):
                r1 = self.parts[n][0]
                j = lax.rem(j_me + k, 4)
                for d, at, dev in ring:
                    src = grads.at[:, pl.ds(pl.multiple_of(lo + (at * 4 + j) * size, 16), size)]
                    self.first[n, k, d] = self.sems.push(src, r1.at[d - 1, k], dev)

    def fold_first(self, k):
        for n, (lo, size, _, cross, i_me, j_me) in enumerate(self.plans):
            r1, s1, r2, _, _ = self.parts[n]
            j = lax.rem(j_me + k, 4)
            for d in (1, 2, 3):
                self.first[n, k, d].wait_recv()
            for s in range(2):
                own = self.grads[s, pl.ds(pl.multiple_of(lo + (i_me * 4 + j) * size, 16), size)]
                total = own.astype(F32)
                for d in (0, 1, 2):
                    total = total + r1[d, k, s].astype(F32)
                s1[k, s] = total.astype(BF16)
            if k:
                dev = [dev for d, _, dev in cross if d == k][0]
                self.second[n, k] = self.sems.push(s1.at[k], r2.at[k - 1], dev)

    def fold_second(self):
        me, push = self.me, self.sems.push
        yh, yl = me["yh"], me["yl"]
        for n in (0, 1):
            _, s1, r2, s2, r3 = self.parts[n]
            for k in (1, 2, 3):
                self.second[n, k].wait_recv()
            for s in range(2):
                total = s1[0, s].astype(F32)
                for d in (0, 1, 2):
                    total = total + r2[d, s].astype(F32)
                s2[s] = total.astype(BF16)
            slot = r3.at[yl * 2 + yh]
            self.third[n, 0] = push(s2.at[1 - yl], slot, device(me, yl=1 - yl))
            self.third[n, 1] = push(s2.at[1 - yl], slot, device(me, yl=1 - yl, yh=1 - yh))
            self.third[n, 2] = push(s2.at[yl], slot, device(me, yh=1 - yh))

    def fold_third(self):
        yh, yl = self.me["yh"], self.me["yl"]
        at = 0
        for n, size in enumerate(self.sizes):
            _, _, _, s2, r3 = self.parts[n]
            r3[yl * 2 + yh] = s2[yl]
            for i in (0, 1, 2):
                self.third[n, i].wait_recv()
            total = r3[0].astype(F32)
            for i in (1, 2, 3):
                total = total + r3[i].astype(F32)
            self.fin[pl.ds(at, size), :] = total.astype(BF16)
            at += size

    def end(self):
        for group in (self.traded, self.first.values(), self.second.values(), self.third.values()):
            for copy in group:
                copy.wait_send()


class Spread:
    COPIES = 30

    def __init__(self, me, sems, local, fin, out, sizes):
        self.sems = sems
        xs = [(d, at, device(me, x=at)) for d, at in around(me, "x")]
        zs = [(d, at, device(me, z=at)) for d, at in around(me, "z")]
        x, z = me["x"], me["z"]
        self.plans = ((0, sizes[0], xs, zs, x, z), (16 * sizes[0], sizes[1], zs, xs, z, x))
        self.out, self.kept, self.cross, self.ring = out, [], {}, {}
        at = 0
        for n, (lo, size, ring, cross, _, j_me) in enumerate(self.plans):
            src = fin.at[pl.ds(at, size)]
            span = self.span(n, j_me)
            copy = pltpu.make_async_copy(src, span, local.at[n])
            copy.start()
            self.kept.append(copy)
            for d, _, dev in cross:
                self.cross[n, d] = sems.push(src, span, dev)
            for d, _, dev in ring:
                self.ring[n, 0, d] = sems.push(src, span, dev)
            at += size

    def span(self, n, j):
        lo, size, _, _, i_me, _ = self.plans[n]
        return self.out.at[pl.ds(pl.multiple_of(lo + (i_me * 4 + j) * size, 16), size)]

    def relay(self):
        for back in (3, 1, 2):
            for n, (_, _, ring, _, _, j_me) in enumerate(self.plans):
                self.cross[n, back].wait_recv()
                span = self.span(n, lax.rem(j_me + 4 - back, 4))
                for d, _, dev in ring:
                    self.ring[n, back, d] = self.sems.push(span, span, dev)

    def end(self):
        for copy in self.ring.values():
            copy.wait_recv()
        for copy in self.kept:
            copy.wait()
        for copy in list(self.cross.values()) + list(self.ring.values()):
            copy.wait_send()


def greet_axes(me):
    flip = 1 - me["yl"]
    greet(
        [device(me, yl=flip), device(me, yl=flip, yh=1 - me["yh"]), device(me, c=1 - me["c"])]
        + [device(me, yh=1 - me["yh"])]
        + [device(me, x=at) for _, at in around(me, "x")]
        + [device(me, z=at) for _, at in around(me, "z")]
    )


def backward_kernel(reduction, *refs):
    refs = list(refs)
    q, do, o, logs, kv, own, flag, left, right, limit = pop(refs, 10)
    operands = pop(refs, len(reduction.operands))
    dq_ref, dkv_own, fin = pop(refs, 3)
    dkv, kk, vv = pop(refs, 3)
    scatter_scratch = pop(refs, len(Scatter.SCRATCH))
    reduce_scratch = pop(refs, len(reduction.scratch))
    send, recv, local = refs
    me = here()
    greet_axes(me)
    sems = Sems(send, recv)
    reduction.bind(me, sems, local, operands, reduce_scratch, fin)
    scatter = Scatter(me, sems, dkv, dkv_own, scatter_scratch)
    flat = dkv.reshape(CTX, 640, 128)

    def one(head, _):
        dq_ref[head] = attend_back_head(
            head, q[head], do[head], o[head], logs[head], kv, own, flag,
            left, right, limit, flat, kk, vv,
        )
        return 0

    reduction.trade()
    reduction.multiply()
    lax.fori_loop(0, KV_HEADS, one, 0)
    scatter.start()
    for k in (1, 3, 2, 0):
        reduction.fold_first(k)
    scatter.middle(0)
    scatter.middle(1)
    reduction.fold_second()
    scatter.last(0)
    scatter.last(1)
    reduction.fold_third()
    scatter.end()
    reduction.end()


def backward(q, do, o, logs, kv, own, plan, reduction, collective_id):
    flags, left, right, limits = plan
    copies = reduction.copies + Scatter.COPIES
    return pl.pallas_call(
        functools.partial(backward_kernel, reduction),
        out_shape=[
            jax.ShapeDtypeStruct((KV_HEADS, ROWS, 128), F32),
            jax.ShapeDtypeStruct((640, 128), F32),
            jax.ShapeDtypeStruct(reduction.fin_shape, BF16),
        ],
        in_specs=[VM] * 10 + [ANY] * len(reduction.operands),
        out_specs=[VM, VM, VM],
        scratch_shapes=[
            pltpu.VMEM((4, 2, 4, 640, 128), BF16),
            pltpu.VMEM((KEYS, 128), BF16),
            pltpu.VMEM((KEYS, 128), BF16),
            *Scatter.SCRATCH,
            *reduction.scratch,
            pltpu.SemaphoreType.DMA((copies,)),
            pltpu.SemaphoreType.DMA((copies,)),
            pltpu.SemaphoreType.DMA((reduction.locals,)),
        ],
        compiler_params=pltpu.CompilerParams(
            collective_id=collective_id, has_side_effects=True, vmem_limit_bytes=BIG
        ),
        name="backward",
    )(
        q, do, o, logs, kv, own, flags, left, right, limits, *reduction.operands,
    )


def finish_kernel(reduction, sizes, *refs):
    refs = list(refs)
    done = refs.pop(0)
    operands = pop(refs, len(reduction.operands))
    out_done, out = pop(refs, 2)
    fin = refs.pop(0)
    reduce_scratch = pop(refs, len(reduction.scratch))
    send, recv, local = refs
    me = here()
    greet_axes(me)
    sems = Sems(send, recv)
    reduction.bind(me, sems, local, operands, reduce_scratch, fin)
    reduction.trade()
    spread = Spread(me, sems, local.at[pl.ds(reduction.locals, 2)], done, out_done, sizes)
    reduction.multiply()
    spread.relay()
    for k in (1, 3, 2, 0):
        reduction.fold_first(k)
    reduction.fold_second()
    reduction.fold_third()
    last = Spread(me, sems, local.at[pl.ds(reduction.locals + 2, 2)], fin, out, reduction.sizes)
    last.relay()
    spread.end()
    last.end()
    reduction.end()


def finish(done, sizes, used, reduction, collective_id):
    copies = reduction.copies + 2 * Spread.COPIES
    return pl.pallas_call(
        functools.partial(finish_kernel, reduction, sizes),
        out_shape=[
            jax.ShapeDtypeStruct((used, 128), BF16),
            jax.ShapeDtypeStruct((reduction.used, 128), BF16),
        ],
        in_specs=[VM] + [ANY] * len(reduction.operands),
        out_specs=[ANY, ANY],
        scratch_shapes=[
            pltpu.VMEM(reduction.fin_shape, BF16),
            *reduction.scratch,
            pltpu.SemaphoreType.DMA((copies,)),
            pltpu.SemaphoreType.DMA((copies,)),
            pltpu.SemaphoreType.DMA((reduction.locals + 4,)),
        ],
        compiler_params=pltpu.CompilerParams(
            collective_id=collective_id, has_side_effects=True, vmem_limit_bytes=BIG
        ),
        name="finish",
    )(done, *reduction.operands)


def low_lanes(rows):
    return lax.broadcasted_iota(jnp.int32, (rows, 128), 1) < HALF


def turn(tile):
    return pltpu.roll(tile, HALF, 1)


def heads_of_tile(tile):
    early, late = tile[:HALF], tile[HALF:]
    low = low_lanes(HALF)
    return jnp.where(low, late, turn(early)), jnp.where(low, turn(late), early)


def tile_of_heads(first, second):
    low = low_lanes(HALF)
    early = jnp.where(low, turn(first), second)
    late = jnp.where(low, first, turn(second))
    return jnp.concatenate([early, late], axis=0)


def put_heads(ref, values):
    for t in range(8):
        if t < 7:
            tile = values[:, t * 128 : (t + 1) * 128]
        else:
            last = values[:, 896:960]
            tile = jnp.concatenate([last, jnp.zeros_like(last)], axis=1)
        for i, block in enumerate(heads_of_tile(tile)):
            head = 2 * t + i
            if head < HEADS:
                at = head % GROUP * HALF
                ref[head // GROUP, at : at + HALF, :] = block.astype(ref.dtype)


def get_heads(ref):
    def block(head):
        if head == HEADS:
            return jnp.zeros((HALF, 128), F32)
        at = head % GROUP * HALF
        return ref[head // GROUP, at : at + HALF, :].astype(F32)

    return [tile_of_heads(block(2 * t), block(2 * t + 1)) for t in range(8)]


def partner(tile):
    lane = lax.broadcasted_iota(jnp.int32, tile.shape, 1)
    return jnp.where(lane % HEAD < 32, pltpu.roll(tile, 96, 1), pltpu.roll(tile, 32, 1))


def inverse_rms(values):
    return lax.rsqrt(jnp.sum(values * values, axis=1, keepdims=True) * (1.0 / D) + EPSILON)


def norm_back(values, inv, gain, grad):
    scaled = grad * gain
    mean = jnp.sum(scaled * values, axis=1, keepdims=True) * (1.0 / D)
    grad_values = inv * scaled - values * (inv * inv * inv) * mean
    return grad_values, jnp.sum(grad * values * inv, axis=0, keepdims=True)


def project_kernel(
    table, tok, gain, w, cosine, sine, q_ref, own_ref, nt_ref, flag, left, right, limit
):
    values = tok[...].astype(F32)
    normed = values * inverse_rms(values) * gain[...]
    low = normed.astype(BF16)
    nt_ref[...] = normed.T.astype(BF16)
    lanes = low_lanes(HALF)
    blocks = []
    for t in range(13):
        u = dot_nn(low, w[:, t * 128 : (t + 1) * 128])
        if t < 10:
            u = u * cosine[...] + partner(u) * sine[...]
        blocks += heads_of_tile(u)
    for head in range(HEADS):
        at = head % GROUP * HALF
        q_ref[head // GROUP, at : at + HALF, :] = blocks[head].astype(BF16)
    for i in range(2 * KV_HEADS):
        own_ref[i * HALF : (i + 1) * HALF, :] = turn(blocks[HEADS + i]).astype(BF16)

    ctx = lax.axis_index("ctx")
    mine = jnp.minimum(table[2 * ctx], table[2 * ctx + 1])
    lane = lax.broadcasted_iota(jnp.int32, (1, 128), 1)
    first = lane < HALF
    offset = lax.rem(lane, HALF)

    def one(i, _):
        early = jnp.minimum(table[2 * i], table[2 * i + 1])
        turn_late = early >= mine
        m = jnp.where(turn_late, 1.0, 0.0)
        row = pl.ds(i, 1)
        flag[row, :] = jnp.where(first, 1.0, m)
        left[row, :] = jnp.where(first, m, 1.0 - m)
        right[row, :] = jnp.where(first, 1.0 - m, 0.0)
        gap = jnp.where(turn_late, mine - early, early - mine)
        blocks_back = jnp.where(first, early - (63 - mine), gap)
        limit[row, :] = (blocks_back * HALF + offset).astype(F32)
        return 0

    lax.fori_loop(0, CTX, one, 0)
    zero = jnp.zeros((1, 128), F32)
    for ref in (flag, left, right):
        ref[CTX:TILES, :] = zero
    limit[CTX:TILES, :] = jnp.where(first, offset, 10**6).astype(F32)


def project(table, tok, gain, w, cosine, sine):
    return pl.pallas_call(
        project_kernel,
        out_shape=[
            jax.ShapeDtypeStruct((KV_HEADS, ROWS, 128), BF16),
            jax.ShapeDtypeStruct((640, 128), BF16),
            jax.ShapeDtypeStruct((D, 128), BF16),
        ]
        + [jax.ShapeDtypeStruct((TILES, 128), F32)] * 4,
        in_specs=[pl.BlockSpec(memory_space=pltpu.SMEM)] + [VM] * 5,
        out_specs=[VM] * 7,
        compiler_params=pltpu.CompilerParams(vmem_limit_bytes=BIG),
        name="project",
    )(table, tok, gain, w, cosine, sine)


def middle_kernel(
    o, tok, cot, gain, out_hbm, gate_hbm, up_hbm, down_hbm,
    layer_out, grad_mid, do_rows, gain_grad, nt, dgu, gt, hid, at_t, gb,
    out_w, gate_w, up_w, down_w, sem,
):
    loads = []
    pairs = ((out_hbm, out_w), (gate_hbm, gate_w), (up_hbm, up_w), (down_hbm, down_w))
    for i, (src, dst) in enumerate(pairs):
        copy = pltpu.make_async_copy(src, dst, sem.at[i])
        copy.start()
        loads.append(copy)
    attended = jnp.concatenate(get_heads(o), axis=1)
    at_t[...] = attended.T[:D].astype(BF16)
    cot_low = cot[...]
    gt[0] = cot_low.astype(F32).T.astype(BF16)
    loads[0].wait()
    middle = tok[...].astype(F32) + dot_nn(attended.astype(BF16)[:, :D], out_w[...])
    inv = inverse_rms(middle)
    normed = middle * inv * gain[...]
    low = normed.astype(BF16)
    nt[...] = normed.T.astype(BF16)
    loads[1].wait()
    gate = dot_nn(low, gate_w[...])
    sigmoid = jax.nn.sigmoid(gate)
    silu = gate * sigmoid
    loads[2].wait()
    up = dot_nn(low, up_w[...])
    hidden = (silu * up).astype(BF16)
    for f in range(4):
        hid[f] = hidden[:, f * 640 : (f + 1) * 640]
    loads[3].wait()
    layer_out[...] = (middle + dot_nn(hidden, down_w[...])).astype(BF16)
    grad_hidden = dot_nt(cot_low, down_w[...])
    grad_gate = (grad_hidden * up * sigmoid * (1.0 + gate * (1.0 - sigmoid))).astype(BF16)
    grad_up = (grad_hidden * silu).astype(BF16)
    dgu[0, :, 0:FF] = grad_gate
    dgu[0, :, FF : 2 * FF] = grad_up
    grad_norm = dot_nt(grad_gate, gate_w[...]) + dot_nt(grad_up, up_w[...])
    grad_values, gain_grad[...] = norm_back(middle, inv, gain[...], grad_norm)
    grad_middle = cot_low.astype(F32) + grad_values
    grad_mid[...] = grad_middle
    branch = grad_middle.astype(BF16)
    gb[0] = jnp.concatenate([branch, jnp.zeros((TOK, 64), BF16)], axis=1)
    put_heads(do_rows, dot_nt(branch, out_w[...]))


def middle(o, tok, cot, gain, out_w, gate_w, up_w, down_w):
    weights = (out_w, gate_w, up_w, down_w)
    return pl.pallas_call(
        middle_kernel,
        out_shape=[
            jax.ShapeDtypeStruct((TOK, D), BF16),
            jax.ShapeDtypeStruct((TOK, D), F32),
            jax.ShapeDtypeStruct((KV_HEADS, ROWS, 128), BF16),
            jax.ShapeDtypeStruct((1, D), F32),
            jax.ShapeDtypeStruct((D, 128), BF16),
            jax.ShapeDtypeStruct((1, TOK, 2 * FF), BF16),
            jax.ShapeDtypeStruct((1, D, 128), BF16),
            jax.ShapeDtypeStruct((4, TOK, 640), BF16),
            jax.ShapeDtypeStruct((D, 128), BF16),
            jax.ShapeDtypeStruct((1, TOK, 1024), BF16),
        ],
        in_specs=[VM] * 4 + [ANY] * 4,
        out_specs=[VM] * 10,
        scratch_shapes=[pltpu.VMEM(w.shape, BF16) for w in weights]
        + [pltpu.SemaphoreType.DMA((4,))],
        compiler_params=pltpu.CompilerParams(vmem_limit_bytes=BIG),
        name="middle",
    )(o, tok, cot, gain, *weights)


def unproject_kernel(dq, dkv, cosine, sine, w, tok, gain, grad_mid, grad_tok, dqkv, gain_grad):
    tiles = get_heads(dq)
    low = low_lanes(TOK)
    turned = [turn(dkv[i * 128 : (i + 1) * 128, :].T) for i in range(5)]
    tiles[7] = jnp.where(low, tiles[7], turned[0])
    for i in range(4):
        tiles.append(jnp.where(low, turned[i], turned[i + 1]))
    tiles.append(jnp.where(low, turned[4], 0.0))
    for t in range(13):
        u = tiles[t]
        if t < 10:
            u = u * cosine[...] - partner(u) * sine[...]
        dqkv[0, :, t * 128 : (t + 1) * 128] = u.astype(BF16)
    grad_norm = dot_nt(dqkv[0], w[...])
    values = tok[...].astype(F32)
    grad_values, gain_grad[...] = norm_back(values, inverse_rms(values), gain[...], grad_norm)
    grad_tok[...] = grad_mid[...] + grad_values


def unproject(dq, dkv, cosine, sine, w, tok, gain, grad_mid):
    return pl.pallas_call(
        unproject_kernel,
        out_shape=[
            jax.ShapeDtypeStruct((TOK, D), F32),
            jax.ShapeDtypeStruct((1, TOK, 1664), BF16),
            jax.ShapeDtypeStruct((1, D), F32),
        ],
        in_specs=[VM] * 8,
        out_specs=[VM] * 3,
        compiler_params=pltpu.CompilerParams(vmem_limit_bytes=BIG),
        name="unproject",
    )(dq, dkv, cosine, sine, w, tok, gain, grad_mid)


def unpack_kernel(g_in, u_in, d_in, o_in, qkv, g, u, d, o, q, k, v):
    step = pl.program_id(0)
    g[...] = g_in[...].astype(F32)
    u[...] = u_in[...].astype(F32)

    @pl.when(step < 5)
    def _():
        d[...] = d_in[...].astype(F32).T

    @pl.when(step < 8)
    def _():
        o[...] = o_in[...].astype(F32)

    @pl.when(step == 0)
    def _():
        tiles = [qkv[t * 240 : (t + 1) * 240, :].astype(F32) for t in range(13)]
        low = low_lanes(240)
        for t in range(7):
            q[:, t * 128 : (t + 1) * 128] = tiles[t]
        q[:, 896:960] = tiles[7][:, :64]
        turned = [turn(t) for t in tiles[7:10]]
        k[:, 0:128] = jnp.where(low, turned[0], turned[1])
        k[:, 128:256] = jnp.where(low, turned[1], turned[2])
        k[:, 256:320] = turned[2][:, :64]
        v[:, 0:128] = tiles[10]
        v[:, 128:256] = tiles[11]
        v[:, 256:320] = tiles[12][:, :64]


def unpack(done, qkv):
    def cut(rows, first, last):
        return pl.BlockSpec((rows, 128), lambda i: (first + jnp.minimum(i, last), 0))

    def out(rows, last):
        return pl.BlockSpec((rows, 128), lambda i: (0, jnp.minimum(i, last)))

    def whole(*shape):
        return pl.BlockSpec(shape, lambda i: (0, 0))

    return pl.pallas_call(
        unpack_kernel,
        grid=(20,),
        out_shape=[
            jax.ShapeDtypeStruct(shape, F32)
            for shape in (
                (240, FF), (240, FF), (640, D), (240, D), (240, D), (240, 320), (240, 320),
            )
        ],
        in_specs=[
            cut(240, 0, 19),
            cut(240, 20, 19),
            cut(960, 10, 4),
            cut(240, 60, 7),
            whole(*qkv.shape),
        ],
        out_specs=[
            out(240, 19),
            out(240, 19),
            pl.BlockSpec((128, D), lambda i: (jnp.minimum(i, 4), 0)),
            out(240, 7),
            whole(240, D),
            whole(240, 320),
            whole(240, 320),
        ],
        compiler_params=pltpu.CompilerParams(vmem_limit_bytes=BIG),
        name="unpack",
    )(done, done, done, done, qkv)


def rope_tables(early):
    row = lax.broadcasted_iota(jnp.int32, (TOK, 128), 0)
    lane = lax.broadcasted_iota(jnp.int32, (TOK, 128), 1)
    block = jnp.where(row < HALF, early, 63 - early)
    position = (block * HALF + row % HALF).astype(F32)
    frequency = BASE ** (-(lane % 32).astype(F32) / 32)
    angles = position * frequency
    return jnp.cos(angles), jnp.where(lane % HEAD < 32, -1.0, 1.0) * jnp.sin(angles)


def swap_rows(a, swap):
    return jnp.where(swap, jnp.concatenate([a[HALF:], a[:HALF]], axis=0), a)


def on_device(
    tokens, cotangent, block_table, attn_gain, w_query, w_key, w_value, w_out, mlp_gain,
    w_gate, w_up, w_down,
):
    ctx = lax.axis_index("ctx")
    gains = jnp.pad(jnp.stack([attn_gain, mlp_gain]), ((0, 14), (0, 16)))
    blank = jnp.zeros((240, 64), BF16)
    qkv_shard = jnp.concatenate([w_query, w_key, w_value, blank], axis=1)
    gains_all, qkv_w = gather_weights((gains, qkv_shard), 0)
    gains_all = gains_all.reshape(4, 16, 256)[:, :2, :240].astype(F32)
    gain_a = gains_all[:, 0].reshape(1, D)
    gain_b = gains_all[:, 1].reshape(1, D)

    own_blocks = lax.dynamic_slice_in_dim(block_table, 2 * ctx, 2)
    swap = own_blocks[0] > own_blocks[1]
    cosine, sine = rope_tables(jnp.min(own_blocks))
    tok = swap_rows(tokens[0], swap)
    cot = swap_rows(cotangent[0], swap)

    q_rows, own_kv, na_t, *plan = project(block_table, tok, gain_a, qkv_w, cosine, sine)
    o_rows, logs, kv, out_w, gate_w, up_w, down_w = forward(
        q_rows, own_kv, plan, (w_out, w_gate, w_up, w_down), 1
    )
    kv = kv.reshape(CTX, 640, 128)
    layer_out, grad_mid, do_rows, grad_gain_b, nb_t, dgu, cot_t, hidden, at_t, branch = middle(
        o_rows, tok, cot, gain_b, out_w, gate_w, up_w, down_w
    )
    ready = Reduction(
        (
            (nb_t.reshape(2, 2, 240, 128), dgu),
            (cot_t, hidden.reshape(2, 2, TOK, 640)),
            (at_t.reshape(2, 2, 240, 128), branch),
        ),
        None,
    )
    dq_rows, dkv, done = backward(q_rows, do_rows, o_rows, logs, kv, own_kv, plan, ready, 2)
    grad_tokens, grad_qkv, grad_gain_a = unproject(
        dq_rows, dkv, cosine, sine, qkv_w, tok, gain_a, grad_mid
    )
    gain_rows = jnp.stack([grad_gain_a, grad_gain_b]).reshape(2, 4, 240).transpose(1, 0, 2)
    gain_rows = jnp.pad(gain_rows, ((0, 0), (0, 0), (0, 16))).reshape(2, 2, 4, 128).astype(BF16)
    gain_rows = jnp.pad(gain_rows, ((0, 0), (0, 0), (0, 12), (0, 0)))
    late = Reduction(((na_t.reshape(2, 2, 240, 128), grad_qkv),), gain_rows)
    flat_done, flat = finish(done, ready.sizes, ready.used, late, 3)
    shard_g, shard_u, shard_d, shard_o, shard_q, shard_k, shard_v = unpack(flat_done, flat)
    shard_gains = flat[3120:3124].reshape(2, 256)[:, :240].astype(F32)
    return (
        swap_rows(layer_out, swap)[None],
        swap_rows(grad_tokens, swap)[None],
        shard_gains[0],
        shard_q,
        shard_k,
        shard_v,
        shard_o,
        shard_gains[1],
        shard_g,
        shard_u,
        shard_d,
    )


def solution(mesh):
    rows, cut = P("fsdp", "ctx", None), P("fsdp", None)
    return jax.shard_map(
        on_device,
        mesh=mesh,
        in_specs=(rows, rows, P(), P("fsdp"), cut, cut, cut, cut, P("fsdp"), cut, cut, cut),
        out_specs=(rows, rows, P("fsdp"), cut, cut, cut, cut, P("fsdp"), cut, cut, cut),
        check_vma=False,
    )
```

profile of v0, /device:TPU:1, one launch (start us, length us, event | category | flops | bytes accessed | tf_op | source)
XLA Modules:
  0.0 344.9 jit_solution(10900061243931307726)
XLA Ops:
  0.6 0.0 copy-start.3
  0.7 1.4 fusion.10
  2.7 0.6 fusion.15
  4.6 0.7 fusion.9
  5.3 0.7 stack.18
  5.9 0.7 stack.19
  6.6 0.6 fusion.8.refs_0_
  7.2 1.0 sine_multiply_fusion
  8.3 1.1 copy.26
  9.3 1.1 copy.27
  10.4 1.1 copy.23
  11.5 0.0 copy-start.1
  11.5 1.2 copy.30
  12.8 1.0 maximum_select_fusion.1
  13.8 0.0 copy-done.3
  13.8 1.1 concatenate.18.refs_1_
  14.9 0.0 copy-done.1
  14.9 1.9 copy.29.refs_3_
  16.8 18.1 %gather_weights.1 = (bf16[64,256]{1,0:T(8,128)(2,1)}, bf16[960,1664]{1,0:T(8,128)(2,1)}) custom-call(bf16[16,256]{1,0:T(8,128)(2,1)} %fusion.8.refs_0_, bf16[240,1664]{1,0:T(8,128)(2,1)} %concatenate.18.refs_1_), custom_call_target="tpu_custom_call" | custom-call | tf_op jit(solution)/shard_map/gather_weights/pallas_call | solution.py:139
  34.9 0.7 slice.86
  35.6 0.7 reshape_squeeze.7.gain
  36.3 0.7 reshape_squeeze.6.gain
  37.0 4.6 %project.1 = (bf16[5,192,128]{2,1,0:T(8,128)(2,1)}, bf16[640,128]{1,0:T(8,128)(2,1)}, bf16[960,128]{1,0:T(8,128)(2,1)}, f32[33,128]{1,0:T(8,128)}, f32[33,128]{1...) custom-call(s32[64]{0:T(128)} %table.1, bf16[128,960]{1,0:T(8,128)(2,1)} %get-tuple-element.122.tok, ...), custom_call_target="tpu_custom_call" | custom-call | tf_op jit(solution)/shard_map/project/pallas_call | solution.py:904
  41.6 68.4 %forward.1 = (f32[5,192,128]{2,1,0:T(8,128)}, f32[5,192,128]{2,1,0:T(8,128)}, bf16[4,2,4,640,128]{4,3,2,1,0:T(8,128)(2,1)}, bf16[960,960]{1,0:T(8,128)(2,1)}, bf...) custom-call(bf16[5,192,128]{2,1,0:T(8,128)(2,1)} %get-tuple-element.54.q_ref.refs_0_, ...), custom_call_target="tpu_custom_call" | custom-call | tf_op jit(solution)/shard_map/forward/pallas_call | solution.py:372
  110.0 14.6 %middle.1 = (bf16[128,960]{1,0:T(8,128)(2,1)}, f32[128,960]{1,0:T(8,128)}, bf16[5,192,128]{2,1,0:T(8,128)(2,1)}, f32[1,960]{1,0:T(1,128)}, bf16[960,128]{1,0:T(8...) custom-call(f32[5,192,128]{2,1,0:T(8,128)} %get-tuple-element.59.o.r, ...), custom_call_target="tpu_custom_call" | custom-call | tf_op jit(solution)/shard_map/middle/pallas_call | solution.py:967
  124.6 128.9 %backward.1 = (f32[5,192,128]{2,1,0:T(8,128)}, f32[640,128]{1,0:T(8,128)}, bf16[1024,128]{1,0:T(8,128)(2,1)}) custom-call(bf16[5,192,128]{2,1,0:T(8,128)(2,1)} %get-tuple-element.54.q_ref.refs_0_, bf16[5,192,128]{2,1,0:T(8,128)(2,1)} %get-tuple-element.65.refs_1_, f32[5,192,128]{2,1,0:T(8,128)} %get-tuple-element.59.o.refs_2_, ...), custom_call_target="tpu_custom_call" | custom-call | tf_op jit(solution)/shard_map/backward/pallas_call | solution.py:717
  253.4 0.0 copy-start.4
  253.4 0.0 copy-start.2
  253.4 5.1 %unproject.1 = (f32[128,960]{1,0:T(8,128)}, bf16[1,128,1664]{2,1,0:T(8,128)(2,1)}, f32[1,960]{1,0:T(1,128)}) custom-call(f32[5,192,128]{2,1,0:T(8,128)} %get-tuple-element.75.dq, f32[640,128]{1,0:T(8,128)} %get-tuple-element.76.dkv, f32[128,128]{1,0:T(8,128)} %get-tuple-element.117.cosine, f32[128,128]{1,0:T(8,128)} %get-tuple-element.116.sine, ...), custom_call_target="tpu_custom_call" | custom-call | tf_op jit(solution)/shard_map/unproject/pallas_call | solution.py:1010
  258.6 0.0 copy-start
  258.6 0.8 convert_reduce_fusion.1
  259.3 0.1 stack.24
  259.4 0.0 copy-done.4
  259.4 0.1 stack.25
  259.6 0.6 pad.15.refs_3_
  260.2 0.0 copy-done.2
  260.2 0.1 fusion.1
  260.3 0.8 copy.35
  261.2 1.1 fusion.11
  262.2 0.0 copy-done
  262.2 0.1 fusion
  262.3 1.0 copy.36
  263.3 58.6 %finish.1 = (bf16[16384,128]{1,0:T(8,128)(2,1)}, bf16[3328,128]{1,0:T(8,128)(2,1)}) custom-call(bf16[1024,128]{1,0:T(8,128)(2,1)} %get-tuple-element.79.refs_0_, bf16[2,2,240,128]{3,2,1,0:T(8,128)(2,1)} %bitcast.35, bf16[1,128,1664]{2,1,0:T(8,128)(2,1)} %get-tuple-element.81.refs_2_, bf16[2,2,16,128]{3,2,1,0:T(8,128)(2,1)} %pad.15.refs_3_), custom_call_target="tpu_custom_call" | custom-call | tf_op jit(solution)/shard_map/finish/pallas_call | solution.py:774
  321.9 0.6 slice.80
  322.6 0.6 fusion.14
  323.2 14.9 %unpack.1 = (f32[240,2560]{1,0:T(8,128)}, f32[240,2560]{1,0:T(8,128)}, f32[640,960]{1,0:T(8,128)}, f32[240,960]{1,0:T(8,128)}, f32[240,960]{1,0:T(8,128)}, /*index=5*/f32[240,320]{1,0:T(8,128)}, f32[240,320]{1,0:T(8,128)}) custom-call(bf16[16384,128]{1,0:T(8,128)(2,1)} %get-tuple-element.85.g_in.u_in.d_in.o_in, ...), custom_call_target="tpu_custom_call" | custom-call | tf_op jit(solution)/shard_map/unpack/pallas_call | solution.py:1063
  338.0 1.9 copy.37
  339.9 1.9 copy.38
  341.8 3.2 copy.39
  (15 shorter events, 0.2 us)
Async XLA Ops:
  0.6 13.1 %copy-start.3 = (bf16[240,960]{1,0:T(8,128)(2,1)S(1)}, bf16[240,960]{1,0:T(8,128)(2,1)}, u32[]{:S(2)}) copy-start(bf16[240,960]{1,0:T(8,128)(2,1)} %param.16) | copy-start | bytes 1382404
  11.5 3.4 copy-start.1
  253.4 6.0 %copy-start.4 = (f32[1,960]{1,0:T(1,128)S(1)}, f32[1,960]{1,0:T(1,128)}, u32[]{:S(2)}) copy-start(f32[1,960]{1,0:T(1,128)} %get-tuple-element.83) | copy-start | bytes 11524
  253.4 6.8 %copy-start.2 = (bf16[128,960]{1,0:T(8,128)(2,1)S(1)}, bf16[128,960]{1,0:T(8,128)(2,1)}, u32[]{:S(2)}) copy-start(bf16[128,960]{1,0:T(8,128)(2,1)} %get-tuple-element.64) | copy-start | bytes 737284
  258.6 3.7 %copy-start = (f32[128,960]{1,0:T(8,128)S(1)}, f32[128,960]{1,0:T(8,128)}, u32[]{:S(2)}) copy-start(f32[128,960]{1,0:T(8,128)} %get-tuple-element.78) | copy-start | bytes 1474564
where the time goes:
time: 348 us; the launch traced here: 345 us
  Pallas kernels  313 us (90%)
  local copies, waits for them, and re-layouts  23.3 us (7%)
  other arithmetic  5.68 us (2%)
    pallas_call x1, Pallas kernels, backward(): pl.pallas_call(functools.partial(backward_kernel, reduction), out_shape=[...  129 us
    pallas_call x1, Pallas kernels, forward(): pl.pallas_call(functools.partial(forward_kernel, n), out_shape=[jax.Shape...  68.4 us
    pallas_call x1, Pallas kernels, finish(): pl.pallas_call(functools.partial(finish_kernel, reduction, sizes), out_sh...  58.6 us
    pallas_call x1, Pallas kernels, gather_weights(): pl.pallas_call(functools.partial(gather_kernel, n), out_shape=gathered(ar...  18.1 us
    unnamed x20, local copies, waits for them, and re-layouts  15 us
    pallas_call x1, Pallas kernels, unpack(): pl.pallas_call(unpack_kernel, grid=(20,), out_shape=[jax.ShapeDtypeStruct...  14.9 us
    pallas_call x1, Pallas kernels, middle(): pl.pallas_call(middle_kernel, out_shape=[jax.ShapeDtypeStruct((TOK, D), B...  14.6 us

commit v1 on v0

--- a/solution.py
+++ b/solution.py
@@ -74,7 +74,7 @@
         return copy
 
 
-def start_gather(me, sems, local, arrays):
+def start_gather(me, sems, local, arrays, stages=None):
     f = me["yl"] * 2 + me["c"]
     near = device(me, yl=1 - me["yl"])
     far = device(me, yl=1 - me["yl"], yh=1 - me["yh"])
@@ -92,9 +92,17 @@
         rows = a.shape[0]
         dst = b.at[pl.ds(pl.multiple_of(f * rows, 16), rows)]
         kept.append(sems.push(a, dst, mate))
-        copy = pltpu.make_async_copy(a, dst, local.at[i])
+        stage = a if stages is None else stages[i]
+        if stages is not None:
+            load = pltpu.make_async_copy(a, stage, local.at[i])
+            load.start()
+        own.append((stage, dst, local.at[i]))
+    if stages is not None:
+        for (a, _), (stage, _, sem) in zip(arrays, own):
+            pltpu.make_async_copy(a, stage, sem).wait()
+    own = [pltpu.make_async_copy(*copy) for copy in own]
+    for copy in own:
         copy.start()
-        own.append(copy)
     return parts, kept, own
 
 
@@ -153,111 +161,238 @@
     )(*arrays)
 
 
-def around(me, axis):
-    return [(d, lax.rem(me[axis] + d, 4)) for d in (1, 3, 2)]
+class Ring:
+    def __init__(self, me, axis):
+        at = me[axis]
+        self.me = at
+        self.right_at, self.opposite_at, self.left_at = (lax.rem(at + d, 4) for d in (1, 2, 3))
+        self.right = device(me, **{axis: self.right_at})
+        self.left = device(me, **{axis: self.left_at})
+        self.opposite = device(me, **{axis: self.opposite_at})
+
+
+class Share:
+    def __init__(self, sems, ring, src, place, halves):
+        self.sems, self.ring, self.place, self.halves = sems, ring, place, halves
+        dst = place(ring.me)
+        self.copies = [sems.push(src, dst, ring.right), sems.push(src, dst, ring.left)]
+        self.passed, self.here = [], False
+        if halves is None:
+            self.passed.append(sems.push(src, dst, ring.opposite))
+
+    def near(self):
+        if not self.here:
+            for copy in self.copies:
+                copy.wait_recv()
+            self.here = True
+
+    def relay(self):
+        self.near()
+        if self.halves is not None:
+            ring, push = self.ring, self.sems.push
+            half = self.halves(self.place(ring.left_at))[0]
+            self.passed.append(push(half, half, ring.right))
+            half = self.halves(self.place(ring.right_at))[1]
+            self.passed.append(push(half, half, ring.left))
+
+    def arrive(self):
+        for copy in self.passed:
+            copy.wait_recv()
+
+    def end(self):
+        for copy in self.copies + self.passed:
+            copy.wait_send()
 
 
 def gather_kv(me, sems, kv, out, once_across):
     x, yh, z = me["x"], me["yh"], me["z"]
     other = device(me, yh=1 - yh)
-    xs = [device(me, x=at) for _, at in around(me, "x")]
-    zs = [device(me, z=at) for _, at in around(me, "z")]
-    key, value = pl.ds(0, 320), pl.ds(320, 320)
-    step1 = [sems.push(kv.at[p], out.at[z, yh, x, p], other) for p in (key, value)]
-    step2 = {}
-    step2[0, 0] = [sems.push(kv.at[key], out.at[z, yh, x, key], dev) for dev in xs]
-    step2[1, 0] = [sems.push(kv.at[value], out.at[z, yh, x, value], dev) for dev in zs]
+    rings = Ring(me, "x"), Ring(me, "z")
+    spans = pl.ds(0, 320), pl.ds(320, 320)
+    across = [sems.push(kv.at[p], out.at[z, yh, x, p], other) for p in spans]
+
+    def near(axis, row, src):
+        lo = 320 * axis
+
+        def place(at):
+            ref = out.at[z, row, at] if axis == 0 else out.at[at, row, x]
+            return ref.at[spans[axis]]
+
+        def halves(ref):
+            return ref.at[pl.ds(0, 160)], ref.at[pl.ds(160, 160)]
+
+        return Share(sems, rings[axis], src, place, halves)
+
+    def far(axis, row):
+        def place(at):
+            return out.at[at, row, :, spans[0]] if axis == 0 else out.at[:, row, at, spans[1]]
+
+        def halves(ref):
+            return ref.at[pl.ds(0, 2)], ref.at[pl.ds(2, 2)]
+
+        src = place(rings[1 - axis].me)
+        return Share(sems, rings[1 - axis], src, place, halves)
+
+    first = [near(axis, yh, kv.at[spans[axis]]) for axis in (0, 1)]
     out[z, yh, x] = kv[...]
-    step3 = []
-    for hop in (0, 1):
-        row = yh if hop == 0 else 1 - yh
-        for axis, (devs, p) in enumerate(((zs, key), (xs, value))):
-            for c in step2[axis, hop]:
-                c.wait_recv()
-            span = out.at[z, row, :, key] if axis == 0 else out.at[:, row, x, value]
-            for dev in devs:
-                step3.append(sems.push(span, span, dev))
-        if hop == 0:
-            for axis, (devs, p) in enumerate(((xs, key), (zs, value))):
-                step1[axis].wait_recv()
-                span = out.at[z, 1 - yh, x, p]
-                step2[axis, 1] = [sems.push(span, span, dev) for dev in devs]
-            once_across()
-    for c in step3:
-        c.wait_recv()
-    return step1 + sum(step2.values(), []) + step3
+    for share in first:
+        share.relay()
+    second = []
+    for axis in (0, 1):
+        across[axis].wait_recv()
+        row = 1 - yh
+        src = out.at[z, row, x, spans[axis]]
+        second.append(near(axis, row, src))
+    once_across()
+    last = []
+    for axis in (0, 1):
+        first[axis].arrive()
+        last.append(far(axis, yh))
+    for share in second:
+        share.relay()
+    for axis in (0, 1):
+        second[axis].arrive()
+        last.append(far(axis, 1 - yh))
+    for share in last:
+        share.relay()
+    for share in last:
+        share.arrive()
+    return across, first + second + last
+
+
+def add_low(a, b):
+    return (a.astype(F32) + b.astype(F32)).astype(BF16)
+
+
+class Fold:
+    def __init__(self, sems, ring, block, landing, passing, direct=False):
+        self.sems, self.ring, self.block, self.direct = sems, ring, block, direct
+        self.landing, self.passing = landing, passing
+        self.copies, self.passed, self.sent = {}, {}, []
+
+    def start_opposite(self, half):
+        ring = self.ring
+        src = self.block(ring.opposite_at, half)
+        dev = ring.opposite if self.direct else (ring.right, ring.left)[half]
+        self.passed[half] = self.sems.push(src, self.passing(half), dev)
+
+    def start_direct(self, half):
+        ring = self.ring
+        at, dev = ((ring.left_at, ring.left), (ring.right_at, ring.right))[half]
+        side = 1 - half
+        self.copies[side, half] = self.sems.push(
+            self.block(at, half), self.landing(side, half), dev
+        )
+
+    def relay(self, half):
+        ring = self.ring
+        at, dev = ((ring.right_at, ring.right), (ring.left_at, ring.left))[half]
+        src = self.block(at, half)
+        if not self.direct:
+            self.passed[half].wait_recv()
+            src[...] = add_low(src[...], self.passing(half)[...])
+        self.copies[half, half] = self.sems.push(src, self.landing(half, half), dev)
+
+    def total(self, half):
+        for side in (0, 1):
+            self.copies[side, half].wait_recv()
+        total = self.block(self.ring.me, half)[...].astype(F32)
+        for side in (0, 1):
+            total = total + self.landing(side, half)[...].astype(F32)
+        if self.direct:
+            self.passed[half].wait_recv()
+            total = total + self.passing(half)[...].astype(F32)
+        return total
+
+    def end(self):
+        for copy in list(self.copies.values()) + list(self.passed.values()):
+            copy.wait_send()
 
 
 class Scatter:
     COPIES = 26
     SCRATCH = [
-        pltpu.VMEM((3, 2, 4, 320, 128), BF16),
-        pltpu.VMEM((3, 2, 4, 320, 128), BF16),
-        pltpu.VMEM((2, 4, 320, 128), BF16),
-        pltpu.VMEM((2, 4, 320, 128), BF16),
-        pltpu.VMEM((3, 2, 320, 128), BF16),
-        pltpu.VMEM((3, 2, 320, 128), BF16),
+        pltpu.VMEM((2, 3, 2, 4, 320, 128), BF16),
+        pltpu.VMEM((2, 2, 4, 320, 128), BF16),
+        pltpu.VMEM((2, 3, 2, 320, 128), BF16),
         pltpu.VMEM((2, 320, 128), BF16),
         pltpu.VMEM((2, 320, 128), BF16),
     ]
 
     def __init__(self, me, sems, part, out, scratch):
         self.me, self.sems, self.part, self.out = me, sems, part, out
-        r1a, r1b, s1a, s1b, r2a, r2b, self.s2, self.r3 = scratch
-        self.r1, self.s1, self.r2 = (r1a, r1b), (s1a, s1b), (r2a, r2b)
-        self.xs = [(d, at, device(me, x=at)) for d, at in around(me, "x")]
-        self.zs = [(d, at, device(me, z=at)) for d, at in around(me, "z")]
-        self.rows = (1 - me["yh"], me["yh"])
-        self.first, self.second, self.third = {}, {}, []
+        self.r1, self.s1, self.r2, self.s2, self.r3 = scratch
+        self.rings = Ring(me, "x"), Ring(me, "z")
+        self.first, self.second, self.third = [], [], []
+        rows = (1 - me["yh"], me["yh"])
+        key, value = pl.ds(0, 320), pl.ds(320, 320)
+
+        def block0(at, half):
+            return part.at[at, rows[half], :, key]
+
+        def block1(at, half):
+            return part.at[:, rows[half], at, value]
+
+        for axis, block in enumerate((block0, block1)):
+            r1, s1, r2 = self.r1, self.s1, self.r2
+            self.first.append(
+                Fold(
+                    sems,
+                    self.rings[1 - axis],
+                    block,
+                    lambda side, half, axis=axis: r1.at[axis, side, half],
+                    lambda half, axis=axis: r1.at[axis, 2, half],
+                )
+            )
+            self.second.append(
+                Fold(
+                    sems,
+                    self.rings[axis],
+                    lambda at, half, axis=axis: s1.at[axis, half, at],
+                    lambda side, half, axis=axis: r2.at[axis, side, half],
+                    lambda half, axis=axis: r2.at[axis, 2, half],
+                )
+            )
 
     def start(self):
-        x, z, part, push = self.me["x"], self.me["z"], self.part, self.sems.push
-        key, value = pl.ds(0, 320), pl.ds(320, 320)
-        for r, row in enumerate(self.rows):
-            for d, at, dev in self.zs:
-                src = part.at[at, row, :, key]
-                self.first[0, r, d] = push(src, self.r1[0].at[d - 1, r], dev)
-            for d, at, dev in self.xs:
-                src = part.at[:, row, at, value]
-                self.first[1, r, d] = push(src, self.r1[1].at[d - 1, r], dev)
-
-    def middle(self, r):
-        x, z, part, row = self.me["x"], self.me["z"], self.part, self.rows[r]
-        for axis in (0, 1):
-            r1, s1, r2 = self.r1[axis], self.s1[axis], self.r2[axis]
-            for d in (1, 2, 3):
-                self.first[axis, r, d].wait_recv()
-            for i in range(4):
-                own = part[z, row, i, 0:320] if axis == 0 else part[i, row, x, 320:640]
-                total = own.astype(F32)
-                for d in (0, 1, 2):
-                    total = total + r1[d, r, i].astype(F32)
-                s1[r, i] = total.astype(BF16)
-            for d, at, dev in (self.xs, self.zs)[axis]:
-                self.second[axis, r, d] = self.sems.push(s1.at[r, at], r2.at[d - 1, r], dev)
-
-    def last(self, r):
+        for half in (0, 1):
+            for fold in self.first:
+                fold.start_opposite(half)
+        for half in (0, 1):
+            for fold in self.first:
+                fold.start_direct(half)
+
+    def relay(self):
+        for half in (0, 1):
+            for fold in self.first:
+                fold.relay(half)
+
+    def middle(self):
+        for half in (0, 1):
+            for axis in (0, 1):
+                self.s1[axis, half] = self.first[axis].total(half).astype(BF16)
+                self.second[axis].start_opposite(half)
+                self.second[axis].start_direct(half)
+        for half in (0, 1):
+            for fold in self.second:
+                fold.relay(half)
+
+    def last(self):
         other = device(self.me, yh=1 - self.me["yh"])
         for axis in (0, 1):
-            s1, r2 = self.s1[axis], self.r2[axis]
-            at = self.me["x"] if axis == 0 else self.me["z"]
-            for d in (1, 2, 3):
-                self.second[axis, r, d].wait_recv()
-            total = s1[r, at].astype(F32)
-            for d in (0, 1, 2):
-                total = total + r2[d, r].astype(F32)
-            if r == 0:
-                self.s2[axis] = total.astype(BF16)
-                self.third.append(self.sems.push(self.s2.at[axis], self.r3.at[axis], other))
-            else:
-                self.out[pl.ds(axis * 320, 320), :] = total
+            self.s2[axis] = self.second[axis].total(0).astype(BF16)
+            self.third.append(self.sems.push(self.s2.at[axis], self.r3.at[axis], other))
+        for axis in (0, 1):
+            self.out[pl.ds(axis * 320, 320), :] = self.second[axis].total(1)
 
     def end(self):
         for axis in (0, 1):
             self.third[axis].wait_recv()
             span = pl.ds(axis * 320, 320)
             self.out[span, :] = self.out[span, :] + self.r3[axis].astype(F32)
-        for c in list(self.first.values()) + list(self.second.values()) + self.third:
+        for fold in self.first + self.second:
+            fold.end()
+        for c in self.third:
             c.wait_send()
 
 
@@ -334,16 +469,16 @@
 def forward_kernel(count, q_ref, own_ref, flag_ref, left_ref, limit_ref, *refs):
     shards, refs = refs[:count], refs[count:]
     o_ref, l_ref, kv_out, *full = refs[: 3 + count]
-    kv, kk, vv, send, recv, local = refs[3 + count :]
+    kv, kk, vv, *stages, send, recv, local = refs[3 + count :]
     me = here()
     greet_axes(me)
     sems = Sems(send, recv)
     started = []
 
     def start_weights():
-        started.extend(start_gather(me, sems, local, list(zip(shards, full))))
-
-    kv_copies = gather_kv(me, sems, own_ref, kv, start_weights)
+        started.extend(start_gather(me, sems, local, list(zip(shards, full)), stages))
+
+    across, shares = gather_kv(me, sems, own_ref, kv, start_weights)
     keep = pltpu.make_async_copy(kv, kv_out, local.at[count])
     keep.start()
     flat = kv.reshape(CTX, 640, 128)
@@ -360,26 +495,29 @@
     relay_gather(me, sems, started)
     lax.fori_loop(3, KV_HEADS, one, 0)
     end_gather(started)
-    for copy in kv_copies:
+    for copy in across:
         copy.wait_send()
+    for share in shares:
+        share.end()
     keep.wait()
 
 
 def forward(q, own, plan, shards, collective_id):
     flags, left, _, limits = plan
     n = len(shards)
-    copies = 5 * n + 26
+    copies = 5 * n + 2 + 8 * 4
     return pl.pallas_call(
         functools.partial(forward_kernel, n),
         out_shape=[jax.ShapeDtypeStruct((KV_HEADS, ROWS, 128), F32)] * 2
         + [jax.ShapeDtypeStruct((4, 2, 4, 640, 128), BF16)]
         + gathered(shards),
-        in_specs=[VM] * (5 + n),
+        in_specs=[VM] * 5 + [ANY] * n,
         out_specs=[VM, VM, ANY] + [ANY] * n,
         scratch_shapes=[
             pltpu.VMEM((4, 2, 4, 640, 128), BF16),
             pltpu.VMEM((KEYS, 128), BF16),
             pltpu.VMEM((KEYS, 128), BF16),
+            *[pltpu.VMEM(a.shape, BF16) for a in shards],
             pltpu.SemaphoreType.DMA((copies,)),
             pltpu.SemaphoreType.DMA((copies,)),
             pltpu.SemaphoreType.DMA((n + 1,)),
@@ -450,8 +588,9 @@
 
 
 class Reduction:
-    def __init__(self, jobs, extra):
+    def __init__(self, jobs, extra, direct=False):
         self.operands, self.jobs, self.scratch, rows = [], [], [], 0
+        self.direct = direct
         for left, right in jobs:
             self.operands += [left, right]
             m, n = left.shape[-2], right.shape[-1]
@@ -477,7 +616,7 @@
                 pltpu.VMEM((4, size, 128), BF16),
             ]
         self.locals = 2 * len(jobs) + 1
-        self.copies = 2 * len(jobs) + 1 + 24 + 6 + 6
+        self.copies = 2 * len(jobs) + 1 + 48 + 12 + 6
         self.fin_shape = (sum(self.sizes), 128)
 
     def bind(self, me, sems, local, operands, scratch, fin):
@@ -496,14 +635,41 @@
             self.extra_buffer = scratch.pop(0)
         self.grads = scratch.pop(0)
         self.parts = [pop(scratch, 5) for _ in self.sizes]
-        xs = [(d, at, device(me, x=at)) for d, at in around(me, "x")]
-        zs = [(d, at, device(me, z=at)) for d, at in around(me, "z")]
-        x, z = me["x"], me["z"]
+        xs, zs = Ring(me, "x"), Ring(me, "z")
         self.plans = (
-            (0, self.sizes[0], xs, zs, x, z),
-            (16 * self.sizes[0], self.sizes[1], zs, xs, z, x),
+            (0, self.sizes[0], xs, zs),
+            (16 * self.sizes[0], self.sizes[1], zs, xs),
         )
         self.first, self.second, self.third = {}, {}, {}
+        for n, (lo, size, ring, cross) in enumerate(self.plans):
+            r1, s1, r2, _, _ = self.parts[n]
+            for k in range(4):
+                j = lax.rem(cross.me + k, 4)
+
+                def block(at, half, lo=lo, size=size, j=j):
+                    start = pl.multiple_of(lo + (at * 4 + j) * size, 16)
+                    return self.grads.at[half, pl.ds(start, size)]
+
+                self.first[n, k] = Fold(
+                    sems,
+                    ring,
+                    block,
+                    lambda side, half, r1=r1, k=k: r1.at[side, k, half],
+                    lambda half, r1=r1, k=k: r1.at[2, k, half],
+                    self.direct,
+                )
+
+            def turned(at, half, s1=s1, cross=cross):
+                return s1.at[lax.rem(at + 4 - cross.me, 4), half]
+
+            self.second[n] = Fold(
+                sems,
+                cross,
+                turned,
+                lambda side, half, r2=r2: r2.at[side, half],
+                lambda half, r2=r2: r2.at[2, half],
+                self.direct,
+            )
 
     def trade(self):
         mate = device(self.me, c=1 - self.me["c"])
@@ -525,29 +691,36 @@
             self.traded.append(push(self.extra_refs[1], self.extra_buffer.at[1], mate))
             keep(self.extra_refs[0], self.extra_buffer.at[0])
 
-    def multiply(self):
-        for copy in self.mine:
+    def multiply(self, job):
+        base = sum(m * (n // 128) for _, m, _, n in self.jobs[:job])
+        for copy in self.mine[2 * job : 2 * job + 2]:
             copy.wait()
-        for copy in self.traded:
+        for copy in self.traded[2 * job : 2 * job + 2]:
             copy.wait_recv()
-        base, grads = 0, self.grads
-        for (_, m, _, n), (lb, rb) in zip(self.jobs, self.buffers):
-            width = 256 if n % 256 == 0 else 128
-            for s in range(2):
-                left = lb[min(s, lb.shape[0] - 1)]
-
-                def block(i, _, left=left, rb=rb, s=s, m=m, width=width, base=base):
-                    at = pl.multiple_of(i * width, 128)
-                    right = rb[min(s, rb.shape[0] - 1), :, pl.ds(at, width)]
-                    result = dot_nn(left, right).astype(BF16)
-                    for w in range(width // 128):
-                        to = pl.multiple_of(base + (i * (width // 128) + w) * m, 16)
-                        grads[s, pl.ds(to, m), :] = result[:, w * 128 : (w + 1) * 128]
-                    return 0
-
-                lax.fori_loop(0, n // width, block, 0)
-            base += m * (n // 128)
+        grads, (_, m, _, n), (lb, rb) = self.grads, self.jobs[job], self.buffers[job]
+        strip = min(n, 1280) if n % 1280 == 0 else n
+        for s in range(2):
+            left = lb[min(s, lb.shape[0] - 1)]
+
+            def block(i, _, left=left, s=s):
+                at = pl.multiple_of(i * strip, 128)
+                right = rb[min(s, rb.shape[0] - 1), :, pl.ds(at, strip)]
+                result = dot_nn(left, right).astype(BF16)
+                for w in range(strip // 128):
+                    to = pl.multiple_of(base + (i * (strip // 128) + w) * m, 16)
+                    grads[s, pl.ds(to, m), :] = result[:, w * 128 : (w + 1) * 128]
+                return 0
+
+            if n == strip:
+                block(0, 0)
+            else:
+                lax.fori_loop(0, n // strip, block, 0)
+
+    def pad(self):
+        base, grads = sum(m * (n // 128) for _, m, _, n in self.jobs), self.grads
         if self.extra:
+            self.mine[-1].wait()
+            self.traded[-1].wait_recv()
             for s in range(2):
                 both = self.extra_buffer[0, s].astype(F32) + self.extra_buffer[1, s].astype(F32)
                 grads[s, pl.ds(base, 16), :] = both.astype(BF16)
@@ -557,42 +730,43 @@
                 grads[s, pl.ds(base, self.used - base), :] = jnp.zeros(
                     (self.used - base, 128), BF16
                 )
-        for k in (1, 3, 2, 0):
-            for n, (lo, size, ring, _, _, j_me) in enumerate(self.plans):
-                r1 = self.parts[n][0]
-                j = lax.rem(j_me + k, 4)
-                for d, at, dev in ring:
-                    src = grads.at[:, pl.ds(pl.multiple_of(lo + (at * 4 + j) * size, 16), size)]
-                    self.first[n, k, d] = self.sems.push(src, r1.at[d - 1, k], dev)
+
+    def start(self, n):
+        for k in (2, 1, 3, 0):
+            for half in (0, 1):
+                self.first[n, k].start_opposite(half)
+        for k in (2, 1, 3, 0):
+            for half in (0, 1):
+                self.first[n, k].start_direct(half)
+
+    def relay(self, k):
+        for half in (0, 1):
+            for n in (0, 1):
+                self.first[n, k].relay(half)
 
     def fold_first(self, k):
-        for n, (lo, size, _, cross, i_me, j_me) in enumerate(self.plans):
-            r1, s1, r2, _, _ = self.parts[n]
-            j = lax.rem(j_me + k, 4)
-            for d in (1, 2, 3):
-                self.first[n, k, d].wait_recv()
-            for s in range(2):
-                own = self.grads[s, pl.ds(pl.multiple_of(lo + (i_me * 4 + j) * size, 16), size)]
-                total = own.astype(F32)
-                for d in (0, 1, 2):
-                    total = total + r1[d, k, s].astype(F32)
-                s1[k, s] = total.astype(BF16)
-            if k:
-                dev = [dev for d, _, dev in cross if d == k][0]
-                self.second[n, k] = self.sems.push(s1.at[k], r2.at[k - 1], dev)
+        for n in (0, 1):
+            s1, second = self.parts[n][1], self.second[n]
+            for half in (0, 1):
+                s1[k, half] = self.first[n, k].total(half).astype(BF16)
+            if k == 2:
+                second.start_opposite(0)
+                second.start_opposite(1)
+            elif k == 1:
+                second.start_direct(1)
+            elif k == 3:
+                second.start_direct(0)
 
     def fold_second(self):
         me, push = self.me, self.sems.push
         yh, yl = me["yh"], me["yl"]
+        for half in (0, 1):
+            for n in (0, 1):
+                self.second[n].relay(half)
         for n in (0, 1):
-            _, s1, r2, s2, r3 = self.parts[n]
-            for k in (1, 2, 3):
-                self.second[n, k].wait_recv()
-            for s in range(2):
-                total = s1[0, s].astype(F32)
-                for d in (0, 1, 2):
-                    total = total + r2[d, s].astype(F32)
-                s2[s] = total.astype(BF16)
+            s2, r3 = self.parts[n][3:]
+            for half in (0, 1):
+                s2[half] = self.second[n].total(half).astype(BF16)
             slot = r3.at[yl * 2 + yh]
             self.third[n, 0] = push(s2.at[1 - yl], slot, device(me, yl=1 - yl))
             self.third[n, 1] = push(s2.at[1 - yl], slot, device(me, yl=1 - yl, yh=1 - yh))
@@ -613,62 +787,85 @@
             at += size
 
     def end(self):
-        for group in (self.traded, self.first.values(), self.second.values(), self.third.values()):
-            for copy in group:
-                copy.wait_send()
+        for fold in list(self.first.values()) + list(self.second.values()):
+            fold.end()
+        for copy in self.traded + list(self.third.values()):
+            copy.wait_send()
 
 
 class Spread:
-    COPIES = 30
-
-    def __init__(self, me, sems, local, fin, out, sizes):
-        self.sems = sems
-        xs = [(d, at, device(me, x=at)) for d, at in around(me, "x")]
-        zs = [(d, at, device(me, z=at)) for d, at in around(me, "z")]
-        x, z = me["x"], me["z"]
-        self.plans = ((0, sizes[0], xs, zs, x, z), (16 * sizes[0], sizes[1], zs, xs, z, x))
-        self.out, self.kept, self.cross, self.ring = out, [], {}, {}
+    COPIES = 40
+
+    def __init__(self, me, sems, local, fin, out, sizes, direct=False):
+        self.direct = direct
+        self.sems, self.out, self.kept, self.cross, self.ring = sems, out, [], [], []
+        xs, zs = Ring(me, "x"), Ring(me, "z")
+        self.plans = ((0, sizes[0], xs, zs), (16 * sizes[0], sizes[1], zs, xs))
         at = 0
-        for n, (lo, size, ring, cross, _, j_me) in enumerate(self.plans):
+        for n, (_, size, ring, cross) in enumerate(self.plans):
             src = fin.at[pl.ds(at, size)]
-            span = self.span(n, j_me)
-            copy = pltpu.make_async_copy(src, span, local.at[n])
+            copy = pltpu.make_async_copy(src, self.span(n, ring.me, cross.me), local.at[n])
             copy.start()
             self.kept.append(copy)
-            for d, _, dev in cross:
-                self.cross[n, d] = sems.push(src, span, dev)
-            for d, _, dev in ring:
-                self.ring[n, 0, d] = sems.push(src, span, dev)
             at += size
-
-    def span(self, n, j):
-        lo, size, _, _, i_me, _ = self.plans[n]
-        return self.out.at[pl.ds(pl.multiple_of(lo + (i_me * 4 + j) * size, 16), size)]
+            self.cross.append(
+                Share(sems, cross, src, functools.partial(self.span, n, ring.me), self.halves(n))
+            )
+            self.share(n, cross.me, src)
+
+    def span(self, n, i, j):
+        lo, size, _, _ = self.plans[n]
+        return self.out.at[pl.ds(pl.multiple_of(lo + (i * 4 + j) * size, 16), size)]
+
+    def halves(self, n):
+        if self.direct:
+            return None
+        size = self.plans[n][1]
+        first = size // 32 * 16
+        return lambda ref: (ref.at[pl.ds(0, first)], ref.at[pl.ds(first, size - first)])
+
+    def share(self, n, j, src=None):
+        ring = self.plans[n][2]
+
+        def place(i):
+            return self.span(n, i, j)
+
+        src = place(ring.me) if src is None else src
+        self.ring.append(Share(self.sems, ring, src, place, self.halves(n)))
 
     def relay(self):
-        for back in (3, 1, 2):
-            for n, (_, _, ring, _, _, j_me) in enumerate(self.plans):
-                self.cross[n, back].wait_recv()
-                span = self.span(n, lax.rem(j_me + 4 - back, 4))
-                for d, _, dev in ring:
-                    self.ring[n, back, d] = self.sems.push(span, span, dev)
+        for n in (0, 1):
+            self.cross[n].relay()
+        for n in (0, 1):
+            cross = self.plans[n][3]
+            self.share(n, cross.left_at)
+            self.share(n, cross.right_at)
+
+    def pass_on(self):
+        self.ring[0].relay()
+        self.ring[1].relay()
+        for n in (0, 1):
+            self.cross[n].arrive()
+            self.share(n, self.plans[n][3].opposite_at)
 
     def end(self):
-        for copy in self.ring.values():
-            copy.wait_recv()
+        for share in self.ring[2:]:
+            share.relay()
+        for share in self.ring:
+            share.arrive()
         for copy in self.kept:
             copy.wait()
-        for copy in list(self.cross.values()) + list(self.ring.values()):
-            copy.wait_send()
-
-
-def greet_axes(me):
+        for share in self.cross + self.ring:
+            share.end()
+
+
+def greet_axes(me, reach=2):
     flip = 1 - me["yl"]
+    rings = Ring(me, "x"), Ring(me, "z")
     greet(
         [device(me, yl=flip), device(me, yl=flip, yh=1 - me["yh"]), device(me, c=1 - me["c"])]
         + [device(me, yh=1 - me["yh"])]
-        + [device(me, x=at) for _, at in around(me, "x")]
-        + [device(me, z=at) for _, at in around(me, "z")]
+        + [dev for ring in rings for dev in (ring.left, ring.right, ring.opposite)[:reach]]
     )
 
 
@@ -677,7 +874,7 @@
     q, do, o, logs, kv, own, flag, left, right, limit = pop(refs, 10)
     operands = pop(refs, len(reduction.operands))
     dq_ref, dkv_own, fin = pop(refs, 3)
-    dkv, kk, vv = pop(refs, 3)
+    kv_here, dkv, kk, vv = pop(refs, 4)
     scatter_scratch = pop(refs, len(Scatter.SCRATCH))
     reduce_scratch = pop(refs, len(reduction.scratch))
     send, recv, local = refs
@@ -685,27 +882,38 @@
     greet_axes(me)
     sems = Sems(send, recv)
     reduction.bind(me, sems, local, operands, reduce_scratch, fin)
+    reduction.trade()
+    load = pltpu.make_async_copy(kv, kv_here, local.at[reduction.locals])
+    load.start()
     scatter = Scatter(me, sems, dkv, dkv_own, scatter_scratch)
     flat = dkv.reshape(CTX, 640, 128)
 
     def one(head, _):
         dq_ref[head] = attend_back_head(
-            head, q[head], do[head], o[head], logs[head], kv, own, flag,
+            head, q[head], do[head], o[head], logs[head], kv_here, own, flag,
             left, right, limit, flat, kk, vv,
         )
         return 0
 
-    reduction.trade()
-    reduction.multiply()
+    reduction.multiply(0)
+    reduction.start(0)
+    reduction.multiply(1)
+    reduction.multiply(2)
+    reduction.pad()
+    reduction.start(1)
+    load.wait()
     lax.fori_loop(0, KV_HEADS, one, 0)
+    for k in (2, 1):
+        reduction.relay(k)
     scatter.start()
-    for k in (1, 3, 2, 0):
+    for k in (3, 0):
+        reduction.relay(k)
+    scatter.relay()
+    for k in (2, 1, 3, 0):
         reduction.fold_first(k)
-    scatter.middle(0)
-    scatter.middle(1)
+    scatter.middle()
     reduction.fold_second()
-    scatter.last(0)
-    scatter.last(1)
+    scatter.last()
     reduction.fold_third()
     scatter.end()
     reduction.end()
@@ -721,9 +929,10 @@
             jax.ShapeDtypeStruct((640, 128), F32),
             jax.ShapeDtypeStruct(reduction.fin_shape, BF16),
         ],
-        in_specs=[VM] * 10 + [ANY] * len(reduction.operands),
+        in_specs=[VM] * 4 + [ANY] + [VM] * 5 + [ANY] * len(reduction.operands),
         out_specs=[VM, VM, VM],
         scratch_shapes=[
+            pltpu.VMEM((CTX, 640, 128), BF16),
             pltpu.VMEM((4, 2, 4, 640, 128), BF16),
             pltpu.VMEM((KEYS, 128), BF16),
             pltpu.VMEM((KEYS, 128), BF16),
@@ -731,7 +940,7 @@
             *reduction.scratch,
             pltpu.SemaphoreType.DMA((copies,)),
             pltpu.SemaphoreType.DMA((copies,)),
-            pltpu.SemaphoreType.DMA((reduction.locals,)),
+            pltpu.SemaphoreType.DMA((reduction.locals + 1,)),
         ],
         compiler_params=pltpu.CompilerParams(
             collective_id=collective_id, has_side_effects=True, vmem_limit_bytes=BIG
@@ -751,19 +960,28 @@
     reduce_scratch = pop(refs, len(reduction.scratch))
     send, recv, local = refs
     me = here()
-    greet_axes(me)
+    greet_axes(me, 3)
     sems = Sems(send, recv)
     reduction.bind(me, sems, local, operands, reduce_scratch, fin)
     reduction.trade()
     spread = Spread(me, sems, local.at[pl.ds(reduction.locals, 2)], done, out_done, sizes)
-    reduction.multiply()
+    reduction.multiply(0)
+    reduction.pad()
+    for n in (0, 1):
+        reduction.start(n)
+    for k in (2, 1, 3, 0):
+        reduction.relay(k)
     spread.relay()
-    for k in (1, 3, 2, 0):
+    for k in (2, 1, 3, 0):
         reduction.fold_first(k)
     reduction.fold_second()
+    spread.pass_on()
     reduction.fold_third()
-    last = Spread(me, sems, local.at[pl.ds(reduction.locals + 2, 2)], fin, out, reduction.sizes)
+    last = Spread(
+        me, sems, local.at[pl.ds(reduction.locals + 2, 2)], fin, out, reduction.sizes, True
+    )
     last.relay()
+    last.pass_on()
     spread.end()
     last.end()
     reduction.end()
@@ -947,8 +1165,13 @@
     for f in range(4):
         hid[f] = hidden[:, f * 640 : (f + 1) * 640]
     loads[3].wait()
-    layer_out[...] = (middle + dot_nn(hidden, down_w[...])).astype(BF16)
-    grad_hidden = dot_nt(cot_low, down_w[...])
+    total = middle
+    for f in range(4):
+        total = total + dot_nt(hidden[:, f * 640 : (f + 1) * 640], down_w[f * D : (f + 1) * D, :])
+    layer_out[...] = total.astype(BF16)
+    grad_hidden = jnp.concatenate(
+        [dot_nn(cot_low, down_w[f * D : (f + 1) * D, :]) for f in range(4)], axis=1
+    )
     grad_gate = (grad_hidden * up * sigmoid * (1.0 + gate * (1.0 - sigmoid))).astype(BF16)
     grad_up = (grad_hidden * silu).astype(BF16)
     dgu[0, :, 0:FF] = grad_gate
@@ -1022,17 +1245,17 @@
 
 
 def unpack_kernel(g_in, u_in, d_in, o_in, qkv, g, u, d, o, q, k, v):
+    for t in range(4):
+        rows, lanes = slice(t * 240, (t + 1) * 240), slice(t * 128, (t + 1) * 128)
+        g[:, lanes] = g_in[rows, :].astype(F32)
+        u[:, lanes] = u_in[rows, :].astype(F32)
+    d[...] = d_in[...].astype(F32)
     step = pl.program_id(0)
-    g[...] = g_in[...].astype(F32)
-    u[...] = u_in[...].astype(F32)
-
-    @pl.when(step < 5)
+
+    @pl.when(step < 4)
     def _():
-        d[...] = d_in[...].astype(F32).T
-
-    @pl.when(step < 8)
-    def _():
-        o[...] = o_in[...].astype(F32)
+        o[:, 0:128] = o_in[0:240, :].astype(F32)
+        o[:, 128:256] = o_in[240:480, :].astype(F32)
 
     @pl.when(step == 0)
     def _():
@@ -1051,36 +1274,30 @@
 
 
 def unpack(done, qkv):
-    def cut(rows, first, last):
-        return pl.BlockSpec((rows, 128), lambda i: (first + jnp.minimum(i, last), 0))
-
-    def out(rows, last):
-        return pl.BlockSpec((rows, 128), lambda i: (0, jnp.minimum(i, last)))
-
     def whole(*shape):
         return pl.BlockSpec(shape, lambda i: (0, 0))
 
     return pl.pallas_call(
         unpack_kernel,
-        grid=(20,),
+        grid=(5,),
         out_shape=[
             jax.ShapeDtypeStruct(shape, F32)
             for shape in (
-                (240, FF), (240, FF), (640, D), (240, D), (240, D), (240, 320), (240, 320),
+                (240, FF), (240, FF), (D, 640), (240, D), (240, D), (240, 320), (240, 320),
             )
         ],
         in_specs=[
-            cut(240, 0, 19),
-            cut(240, 20, 19),
-            cut(960, 10, 4),
-            cut(240, 60, 7),
+            pl.BlockSpec((960, 128), lambda i: (i, 0)),
+            pl.BlockSpec((960, 128), lambda i: (5 + i, 0)),
+            pl.BlockSpec((960, 128), lambda i: (10 + i, 0)),
+            pl.BlockSpec((480, 128), lambda i: (30 + jnp.minimum(i, 3), 0)),
             whole(*qkv.shape),
         ],
         out_specs=[
-            out(240, 19),
-            out(240, 19),
-            pl.BlockSpec((128, D), lambda i: (jnp.minimum(i, 4), 0)),
-            out(240, 7),
+            pl.BlockSpec((240, 512), lambda i: (0, i)),
+            pl.BlockSpec((240, 512), lambda i: (0, i)),
+            pl.BlockSpec((D, 128), lambda i: (0, i)),
+            pl.BlockSpec((240, 256), lambda i: (0, jnp.minimum(i, 3))),
             whole(240, D),
             whole(240, 320),
             whole(240, 320),
@@ -1125,7 +1342,7 @@
 
     q_rows, own_kv, na_t, *plan = project(block_table, tok, gain_a, qkv_w, cosine, sine)
     o_rows, logs, kv, out_w, gate_w, up_w, down_w = forward(
-        q_rows, own_kv, plan, (w_out, w_gate, w_up, w_down), 1
+        q_rows, own_kv, plan, (w_out, w_gate, w_up, w_down.T), 1
     )
     kv = kv.reshape(CTX, 640, 128)
     layer_out, grad_mid, do_rows, grad_gain_b, nb_t, dgu, cot_t, hidden, at_t, branch = middle(
@@ -1146,7 +1363,7 @@
     gain_rows = jnp.stack([grad_gain_a, grad_gain_b]).reshape(2, 4, 240).transpose(1, 0, 2)
     gain_rows = jnp.pad(gain_rows, ((0, 0), (0, 0), (0, 16))).reshape(2, 2, 4, 128).astype(BF16)
     gain_rows = jnp.pad(gain_rows, ((0, 0), (0, 0), (0, 12), (0, 0)))
-    late = Reduction(((na_t.reshape(2, 2, 240, 128), grad_qkv),), gain_rows)
+    late = Reduction(((na_t.reshape(2, 2, 240, 128), grad_qkv),), gain_rows, True)
     flat_done, flat = finish(done, ready.sizes, ready.used, late, 3)
     shard_g, shard_u, shard_d, shard_o, shard_q, shard_k, shard_v = unpack(flat_done, flat)
     shard_gains = flat[3120:3124].reshape(2, 256)[:, :240].astype(F32)
@@ -1161,7 +1378,7 @@
         shard_gains[1],
         shard_g,
         shard_u,
-        shard_d,
+        shard_d.T,
     )
 
 

time: 348 us -> 296 us (0.85)
  Pallas kernels: 313 us -> 267 us
  local copies, waits for them, and re-layouts: 23.3 us -> 18.2 us
    pallas_call x1, Pallas kernels: 129 us -> 104 us  [backward(): pl.pallas_call(functools.partial(backward_kernel, reduction), out_shape=[...]
    pallas_call x1, Pallas kernels: 58.6 us -> 47.9 us  [finish(): pl.pallas_call(functools.partial(finish_kernel, reduction, sizes), out_sh...]
    pallas_call x1, Pallas kernels: 14.9 us -> 8.16 us  [unpack(): pl.pallas_call(unpack_kernel, grid=(5,), out_shape=[jax.ShapeDtypeStruct(...]
    unnamed x20 -> x16, local copies, waits for them, and re-layouts: 15 us -> 9.88 us
where the time goes in v1:
time: 296 us; the launch traced here: 294 us
  Pallas kernels  267 us (90%)
  local copies, waits for them, and re-layouts  18.2 us (6%)
  other arithmetic  5.67 us (2%)
    pallas_call x1, Pallas kernels, backward(): pl.pallas_call(functools.partial(backward_kernel, reduction), out_shape=[...  104 us
    pallas_call x1, Pallas kernels, forward(): pl.pallas_call(functools.partial(forward_kernel, n), out_shape=[jax.Shape...  65.1 us
    pallas_call x1, Pallas kernels, finish(): pl.pallas_call(functools.partial(finish_kernel, reduction, sizes), out_sh...  47.9 us
    pallas_call x1, Pallas kernels, gather_weights(): pl.pallas_call(functools.partial(gather_kernel, n), out_shape=gathered(ar...  18.1 us
    pallas_call x1, Pallas kernels, middle(): pl.pallas_call(middle_kernel, out_shape=[jax.ShapeDtypeStruct((TOK, D), B...  14.4 us
    unnamed x16, local copies, waits for them, and re-layouts  9.88 us
    pallas_call x1, Pallas kernels, unpack(): pl.pallas_call(unpack_kernel, grid=(5,), out_shape=[jax.ShapeDtypeStruct(...  8.16 us

profile of v1, /device:TPU:1, one launch (start us, length us, event | category | flops | bytes accessed | tf_op | source)
XLA Modules:
  0.0 294.0 jit_solution(16383594698122802253)
XLA Ops:
  0.6 0.0 copy-start.2
  0.7 1.4 fusion.10
  2.7 0.6 fusion.15
  4.6 0.7 fusion.9
  5.3 0.7 stack.18
  5.9 0.7 stack.19
  6.6 0.6 fusion.8.refs_0_
  7.2 1.0 sine_multiply_fusion
  8.2 1.1 copy.26
  9.3 1.1 copy.27
  10.4 1.1 copy.23
  11.5 1.1 copy.29
  12.6 1.0 maximum_select_fusion.1
  13.6 0.0 copy-done.2
  13.7 1.1 concatenate.18.refs_1_
  14.8 18.1 %gather_weights.1 = (bf16[64,256]{1,0:T(8,128)(2,1)}, bf16[960,1664]{1,0:T(8,128)(2,1)}) custom-call(bf16[16,256]{1,0:T(8,128)(2,1)} %fusion.8.refs_0_, bf16[240,1664]{1,0:T(8,128)(2,1)} %concatenate.18.refs_1_), custom_call_target="tpu_custom_call" | custom-call | tf_op jit(solution)/shard_map/gather_weights/pallas_call | solution.py:147
  32.9 0.7 slice.86
  33.6 0.7 reshape_squeeze.7.gain
  34.3 0.7 reshape_squeeze.6.gain
  35.0 4.6 %project.1 = (bf16[5,192,128]{2,1,0:T(8,128)(2,1)}, bf16[640,128]{1,0:T(8,128)(2,1)}, bf16[960,128]{1,0:T(8,128)(2,1)}, f32[33,128]{1,0:T(8,128)}, f32[33,128]{1...) custom-call(s32[64]{0:T(128)} %table.1, bf16[128,960]{1,0:T(8,128)(2,1)} %get-tuple-element.122.tok, ...), custom_call_target="tpu_custom_call" | custom-call | tf_op jit(solution)/shard_map/project/pallas_call | solution.py:1122
  39.5 65.1 %forward.1 = (f32[5,192,128]{2,1,0:T(8,128)}, f32[5,192,128]{2,1,0:T(8,128)}, bf16[4,2,4,640,128]{4,3,2,1,0:T(8,128)(2,1)}, bf16[960,960]{1,0:T(8,128)(2,1)}, bf...) custom-call(bf16[5,192,128]{2,1,0:T(8,128)(2,1)} %get-tuple-element.54.q_ref.refs_0_, ...), custom_call_target="tpu_custom_call" | custom-call | tf_op jit(solution)/shard_map/forward/pallas_call | solution.py:509
  104.6 14.4 %middle.1 = (bf16[128,960]{1,0:T(8,128)(2,1)}, f32[128,960]{1,0:T(8,128)}, bf16[5,192,128]{2,1,0:T(8,128)(2,1)}, f32[1,960]{1,0:T(1,128)}, bf16[960,128]{1,0:T(8...) custom-call(f32[5,192,128]{2,1,0:T(8,128)} %get-tuple-element.59.o.r, ...), custom_call_target="tpu_custom_call" | custom-call | tf_op jit(solution)/shard_map/middle/pallas_call | solution.py:1190
  119.1 104.0 %backward.1 = (f32[5,192,128]{2,1,0:T(8,128)}, f32[640,128]{1,0:T(8,128)}, bf16[1024,128]{1,0:T(8,128)(2,1)}) custom-call(bf16[5,192,128]{2,1,0:T(8,128)(2,1)} %get-tuple-element.54.q_ref.refs_0_, bf16[5,192,128]{2,1,0:T(8,128)(2,1)} %get-tuple-element.65.refs_1_, f32[5,192,128]{2,1,0:T(8,128)} %get-tuple-element.59.o.refs_2_, ...), custom_call_target="tpu_custom_call" | custom-call | tf_op jit(solution)/shard_map/backward/pallas_call | solution.py:925
  223.0 0.0 copy-start.3
  223.0 0.0 copy-start.1
  223.1 5.1 %unproject.1 = (f32[128,960]{1,0:T(8,128)}, bf16[1,128,1664]{2,1,0:T(8,128)(2,1)}, f32[1,960]{1,0:T(1,128)}) custom-call(f32[5,192,128]{2,1,0:T(8,128)} %get-tuple-element.75.dq, f32[640,128]{1,0:T(8,128)} %get-tuple-element.76.dkv, f32[128,128]{1,0:T(8,128)} %get-tuple-element.117.cosine, f32[128,128]{1,0:T(8,128)} %get-tuple-element.116.sine, ...), custom_call_target="tpu_custom_call" | custom-call | tf_op jit(solution)/shard_map/unproject/pallas_call | solution.py:1233
  228.2 0.0 copy-start
  228.2 0.8 convert_reduce_fusion.1
  228.9 0.1 stack.24
  229.0 0.0 copy-done.3
  229.0 0.1 stack.25
  229.2 0.6 pad.15.refs_3_
  229.8 0.0 copy-done.1
  229.8 0.1 fusion.1
  229.9 0.8 copy.34
  230.8 1.1 fusion.11
  231.8 0.0 copy-done
  231.8 0.1 fusion
  231.9 1.0 copy.35
  232.9 47.9 %finish.1 = (bf16[16384,128]{1,0:T(8,128)(2,1)}, bf16[3328,128]{1,0:T(8,128)(2,1)}) custom-call(bf16[1024,128]{1,0:T(8,128)(2,1)} %get-tuple-element.79.refs_0_, bf16[2,2,240,128]{3,2,1,0:T(8,128)(2,1)} %bitcast.38, bf16[1,128,1664]{2,1,0:T(8,128)(2,1)} %get-tuple-element.81.refs_2_, bf16[2,2,16,128]{3,2,1,0:T(8,128)(2,1)} %pad.15.refs_3_), custom_call_target="tpu_custom_call" | custom-call | tf_op jit(solution)/shard_map/finish/pallas_call | solution.py:992
  280.8 0.7 slice.80
  281.5 0.6 fusion.14
  282.1 8.2 %unpack.1 = (f32[240,2560]{1,0:T(8,128)}, f32[240,2560]{1,0:T(8,128)}, f32[960,640]{1,0:T(8,128)}, f32[240,960]{1,0:T(8,128)}, f32[240,960]{1,0:T(8,128)}, /*index=5*/f32[240,320]{1,0:T(8,128)}, f32[240,320]{1,0:T(8,128)}) custom-call(bf16[16384,128]{1,0:T(8,128)(2,1)} %get-tuple-element.85.g_in.u_in.d_in.o_in, ...), custom_call_target="tpu_custom_call" | custom-call | tf_op jit(solution)/shard_map/unpack/pallas_call | solution.py:1280
  290.3 1.9 copy.36
  292.1 1.9 copy.37
  (15 shorter events, 0.2 us)
Async XLA Ops:
  0.6 13.0 %copy-start.2 = (bf16[240,960]{1,0:T(8,128)(2,1)S(1)}, bf16[240,960]{1,0:T(8,128)(2,1)}, u32[]{:S(2)}) copy-start(bf16[240,960]{1,0:T(8,128)(2,1)} %param.16) | copy-start | bytes 1382404
  223.0 6.0 %copy-start.3 = (f32[1,960]{1,0:T(1,128)S(1)}, f32[1,960]{1,0:T(1,128)}, u32[]{:S(2)}) copy-start(f32[1,960]{1,0:T(1,128)} %get-tuple-element.83) | copy-start | bytes 11524
  223.0 6.8 %copy-start.1 = (bf16[128,960]{1,0:T(8,128)(2,1)S(1)}, bf16[128,960]{1,0:T(8,128)(2,1)}, u32[]{:S(2)}) copy-start(bf16[128,960]{1,0:T(8,128)(2,1)} %get-tuple-element.64) | copy-start | bytes 737284
  228.2 3.7 %copy-start = (f32[128,960]{1,0:T(8,128)S(1)}, f32[128,960]{1,0:T(8,128)}, u32[]{:S(2)}) copy-start(f32[128,960]{1,0:T(8,128)} %get-tuple-element.78) | copy-start | bytes 1474564

commit v2 on v1

--- a/solution.py
+++ b/solution.py
@@ -234,6 +234,7 @@
         return Share(sems, rings[1 - axis], src, place, halves)
 
     first = [near(axis, yh, kv.at[spans[axis]]) for axis in (0, 1)]
+    once_across()
     out[z, yh, x] = kv[...]
     for share in first:
         share.relay()
@@ -243,7 +244,6 @@
         row = 1 - yh
         src = out.at[z, row, x, spans[axis]]
         second.append(near(axis, row, src))
-    once_across()
     last = []
     for axis in (0, 1):
         first[axis].arrive()
@@ -587,8 +587,108 @@
     return taken
 
 
+class Column:
+    COPIES = 24
+
+    @staticmethod
+    def scratch(pc):
+        return [
+            pltpu.VMEM((3, 4, 4 * pc, 128), BF16),
+            pltpu.VMEM((4, 4 * pc, 128), BF16),
+            pltpu.VMEM((3, 2, 2 * pc, 128), BF16),
+            pltpu.VMEM((4 * pc, 128), BF16),
+            pltpu.VMEM((3, 2, pc // 2, 128), BF16),
+        ]
+
+    def __init__(self, me, sems, grads, lo, pc, scratch, fin):
+        self.me, self.sems, self.grads, self.lo, self.pc, self.fin = me, sems, grads, lo, pc, fin
+        self.ry, self.sy, rx, self.sx, rz = scratch
+        self.first = {}
+        sy, sx, x = self.sy, self.sx, me["x"]
+
+        def strip(at, half):
+            return sy.at[lax.rem(at + 4 - x, 4), pl.ds(half * 2 * pc, 2 * pc)]
+
+        def piece(at, half):
+            return sx.at[pl.ds(pl.multiple_of(at * pc + half * (pc // 2), 16), pc // 2)]
+
+        self.over_x = Fold(
+            sems,
+            Ring(me, "x"),
+            strip,
+            lambda side, half: rx.at[side, half],
+            lambda half: rx.at[2, half],
+        )
+        self.over_z = Fold(
+            sems,
+            Ring(me, "z"),
+            piece,
+            lambda side, half: rz.at[side, half],
+            lambda half: rz.at[2, half],
+        )
+
+    def rows(self, half, k):
+        i = lax.rem(self.me["x"] + k, 4)
+        start = pl.multiple_of(self.lo + (half * 16 + i * 4) * self.pc, 16)
+        return pl.ds(start, 4 * self.pc)
+
+    def start(self):
+        me = self.me
+        yl, yh = me["yl"], me["yh"]
+        ways = (
+            (1 - yl, yh, device(me, yl=1 - yl)),
+            (1 - yl, 1 - yh, device(me, yl=1 - yl, yh=1 - yh)),
+            (yl, 1 - yh, device(me, yh=1 - yh)),
+        )
+        for k in (2, 1, 3, 0):
+            for slot, (shard, half, dev) in enumerate(ways):
+                src = self.grads.at[shard, self.rows(half, k)]
+                self.first[k, slot] = self.sems.push(src, self.ry.at[slot, k], dev)
+
+    def fold_first(self, k):
+        for slot in (0, 1, 2):
+            self.first[k, slot].wait_recv()
+        total = self.grads[self.me["yl"], self.rows(self.me["yh"], k)].astype(F32)
+        for slot in (0, 1, 2):
+            total = total + self.ry[slot, k].astype(F32)
+        self.sy[k] = total.astype(BF16)
+        if k == 2:
+            self.over_x.start_opposite(0)
+            self.over_x.start_opposite(1)
+        elif k == 1:
+            self.over_x.start_direct(1)
+        elif k == 3:
+            self.over_x.start_direct(0)
+
+    def relay(self):
+        self.over_x.relay(0)
+        self.over_x.relay(1)
+
+    def fold_second(self):
+        for half in (0, 1):
+            span = pl.ds(half * 2 * self.pc, 2 * self.pc)
+            self.sx[span] = self.over_x.total(half).astype(BF16)
+        for half in (0, 1):
+            self.over_z.start_opposite(half)
+            self.over_z.start_direct(half)
+
+    def fold_third(self):
+        self.over_z.relay(0)
+        self.over_z.relay(1)
+
+    def end(self):
+        base = self.fin.shape[0] - self.pc
+        for half in (0, 1):
+            span = pl.ds(base + half * (self.pc // 2), self.pc // 2)
+            self.fin[span, :] = self.over_z.total(half).astype(BF16)
+        self.over_x.end()
+        self.over_z.end()
+        for copy in self.first.values():
+            copy.wait_send()
+
+
 class Reduction:
-    def __init__(self, jobs, extra, direct=False):
+    def __init__(self, jobs, extra, direct=False, pc=0):
         self.operands, self.jobs, self.scratch, rows = [], [], [], 0
         self.direct = direct
         for left, right in jobs:
@@ -603,9 +703,10 @@
             self.operands.append(extra)
             self.scratch.append(pltpu.VMEM((2, 2, 16, 128), BF16))
             rows += 16
-        pieces = -(-rows // 256)
+        pieces = -(-rows // 256) - pc // 8
         self.sizes = ((pieces + 1) // 2 * 16, pieces // 2 * 16)
-        self.used = 16 * sum(self.sizes)
+        self.pc = pc
+        self.used = 16 * (sum(self.sizes) + 2 * pc)
         self.scratch.append(pltpu.VMEM((2, self.used, 128), BF16))
         for size in self.sizes:
             self.scratch += [
@@ -617,7 +718,10 @@
             ]
         self.locals = 2 * len(jobs) + 1
         self.copies = 2 * len(jobs) + 1 + 48 + 12 + 6
-        self.fin_shape = (sum(self.sizes), 128)
+        self.fin_shape = (sum(self.sizes) + pc, 128)
+        if pc:
+            self.scratch += Column.scratch(pc)
+            self.copies += Column.COPIES
 
     def bind(self, me, sems, local, operands, scratch, fin):
         operands, scratch = list(operands), list(scratch)
@@ -635,6 +739,9 @@
             self.extra_buffer = scratch.pop(0)
         self.grads = scratch.pop(0)
         self.parts = [pop(scratch, 5) for _ in self.sizes]
+        if self.pc:
+            lo = 16 * sum(self.sizes)
+            self.column = Column(me, sems, self.grads, lo, self.pc, scratch, fin)
         xs, zs = Ring(me, "x"), Ring(me, "z")
         self.plans = (
             (0, self.sizes[0], xs, zs),
@@ -794,28 +901,45 @@
 
 
 class Spread:
-    COPIES = 40
-
-    def __init__(self, me, sems, local, fin, out, sizes, direct=False):
-        self.direct = direct
-        self.sems, self.out, self.kept, self.cross, self.ring = sems, out, [], [], []
+    COPIES = 81
+
+    def __init__(self, me, sems, local, fin, out, sizes, direct=False, pc=0, other=None):
+        self.direct, self.fin, self.pc, self.other = direct, fin, pc, other
+        self.sems, self.local, self.out = sems, local, out
+        self.kept, self.cross, self.own, self.near, self.far = [], [], [], [], []
         xs, zs = Ring(me, "x"), Ring(me, "z")
-        self.plans = ((0, sizes[0], xs, zs), (16 * sizes[0], sizes[1], zs, xs))
+        base, yh = 16 * sum(sizes), me["yh"]
+        self.plans = [(0, sizes[0], xs, zs), (16 * sizes[0], sizes[1], zs, xs)]
+        self.swap = None
+        if pc:
+            self.plans.append((base + yh * (16 * pc), pc, xs, zs))
+            self.plans.append((base + (1 - yh) * (16 * pc), pc, zs, xs))
+            src = fin.at[pl.ds(sum(sizes), pc)]
+            self.swap = sems.push(src, other, device(me, yh=1 - yh))
         at = 0
-        for n, (_, size, ring, cross) in enumerate(self.plans):
-            src = fin.at[pl.ds(at, size)]
-            copy = pltpu.make_async_copy(src, self.span(n, ring.me, cross.me), local.at[n])
-            copy.start()
-            self.kept.append(copy)
+        for n in range(3 if pc else 2):
+            size = self.plans[n][1]
+            self.begin(n, fin.at[pl.ds(at, size)])
             at += size
-            self.cross.append(
-                Share(sems, cross, src, functools.partial(self.span, n, ring.me), self.halves(n))
-            )
-            self.share(n, cross.me, src)
+
+    def begin(self, n, src):
+        _, _, ring, cross = self.plans[n]
+        copy = pltpu.make_async_copy(src, self.span(n, ring.me, cross.me), self.local.at[n])
+        copy.start()
+        self.kept.append(copy)
+        place = functools.partial(self.span, n, ring.me)
+        self.cross.append(Share(self.sems, cross, src, place, self.halves(n)))
+        self.own.append(self.share(n, cross.me, src))
+
+    def across(self):
+        if self.pc:
+            self.swap.wait_recv()
+            self.begin(3, self.other)
 
     def span(self, n, i, j):
         lo, size, _, _ = self.plans[n]
-        return self.out.at[pl.ds(pl.multiple_of(lo + (i * 4 + j) * size, 16), size)]
+        at = j * 4 + i if n == 3 else i * 4 + j
+        return self.out.at[pl.ds(pl.multiple_of(lo + at * size, 16), size)]
 
     def halves(self, n):
         if self.direct:
@@ -831,32 +955,33 @@
             return self.span(n, i, j)
 
         src = place(ring.me) if src is None else src
-        self.ring.append(Share(self.sems, ring, src, place, self.halves(n)))
+        return Share(self.sems, ring, src, place, self.halves(n))
 
     def relay(self):
-        for n in (0, 1):
-            self.cross[n].relay()
-        for n in (0, 1):
-            cross = self.plans[n][3]
-            self.share(n, cross.left_at)
-            self.share(n, cross.right_at)
+        for share in self.cross:
+            share.relay()
+        for n, plan in enumerate(self.plans):
+            self.near.append(self.share(n, plan[3].left_at))
+            self.near.append(self.share(n, plan[3].right_at))
 
     def pass_on(self):
-        self.ring[0].relay()
-        self.ring[1].relay()
-        for n in (0, 1):
+        for share in self.own:
+            share.relay()
+        for n, plan in enumerate(self.plans):
             self.cross[n].arrive()
-            self.share(n, self.plans[n][3].opposite_at)
+            self.far.append(self.share(n, plan[3].opposite_at))
 
     def end(self):
-        for share in self.ring[2:]:
+        for share in self.near + self.far:
             share.relay()
-        for share in self.ring:
+        for share in self.own + self.near + self.far:
             share.arrive()
         for copy in self.kept:
             copy.wait()
-        for share in self.cross + self.ring:
+        for share in self.cross + self.own + self.near + self.far:
             share.end()
+        if self.pc:
+            self.swap.wait_send()
 
 
 def greet_axes(me, reach=2):
@@ -895,12 +1020,14 @@
         )
         return 0
 
+    column = reduction.column
     reduction.multiply(0)
     reduction.start(0)
     reduction.multiply(1)
+    reduction.start(1)
     reduction.multiply(2)
     reduction.pad()
-    reduction.start(1)
+    column.start()
     load.wait()
     lax.fori_loop(0, KV_HEADS, one, 0)
     for k in (2, 1):
@@ -908,14 +1035,20 @@
     scatter.start()
     for k in (3, 0):
         reduction.relay(k)
+    for k in (2, 1, 3, 0):
+        column.fold_first(k)
     scatter.relay()
     for k in (2, 1, 3, 0):
         reduction.fold_first(k)
+    column.relay()
     scatter.middle()
     reduction.fold_second()
+    column.fold_second()
     scatter.last()
     reduction.fold_third()
+    column.fold_third()
     scatter.end()
+    column.end()
     reduction.end()
 
 
@@ -951,12 +1084,12 @@
     )
 
 
-def finish_kernel(reduction, sizes, *refs):
+def finish_kernel(reduction, sizes, pc, *refs):
     refs = list(refs)
     done = refs.pop(0)
     operands = pop(refs, len(reduction.operands))
     out_done, out = pop(refs, 2)
-    fin = refs.pop(0)
+    fin, other = pop(refs, 2)
     reduce_scratch = pop(refs, len(reduction.scratch))
     send, recv, local = refs
     me = here()
@@ -964,13 +1097,15 @@
     sems = Sems(send, recv)
     reduction.bind(me, sems, local, operands, reduce_scratch, fin)
     reduction.trade()
-    spread = Spread(me, sems, local.at[pl.ds(reduction.locals, 2)], done, out_done, sizes)
+    slots = local.at[pl.ds(reduction.locals, 4)]
+    spread = Spread(me, sems, slots, done, out_done, sizes, False, pc, other)
     reduction.multiply(0)
     reduction.pad()
     for n in (0, 1):
         reduction.start(n)
     for k in (2, 1, 3, 0):
         reduction.relay(k)
+    spread.across()
     spread.relay()
     for k in (2, 1, 3, 0):
         reduction.fold_first(k)
@@ -978,7 +1113,7 @@
     spread.pass_on()
     reduction.fold_third()
     last = Spread(
-        me, sems, local.at[pl.ds(reduction.locals + 2, 2)], fin, out, reduction.sizes, True
+        me, sems, local.at[pl.ds(reduction.locals + 4, 2)], fin, out, reduction.sizes, True
     )
     last.relay()
     last.pass_on()
@@ -987,22 +1122,23 @@
     reduction.end()
 
 
-def finish(done, sizes, used, reduction, collective_id):
+def finish(done, ready, reduction, collective_id):
     copies = reduction.copies + 2 * Spread.COPIES
     return pl.pallas_call(
-        functools.partial(finish_kernel, reduction, sizes),
+        functools.partial(finish_kernel, reduction, ready.sizes, ready.pc),
         out_shape=[
-            jax.ShapeDtypeStruct((used, 128), BF16),
+            jax.ShapeDtypeStruct((ready.used, 128), BF16),
             jax.ShapeDtypeStruct((reduction.used, 128), BF16),
         ],
         in_specs=[VM] + [ANY] * len(reduction.operands),
         out_specs=[ANY, ANY],
         scratch_shapes=[
             pltpu.VMEM(reduction.fin_shape, BF16),
+            pltpu.VMEM((ready.pc, 128), BF16),
             *reduction.scratch,
             pltpu.SemaphoreType.DMA((copies,)),
             pltpu.SemaphoreType.DMA((copies,)),
-            pltpu.SemaphoreType.DMA((reduction.locals + 4,)),
+            pltpu.SemaphoreType.DMA((reduction.locals + 6,)),
         ],
         compiler_params=pltpu.CompilerParams(
             collective_id=collective_id, has_side_effects=True, vmem_limit_bytes=BIG
@@ -1289,8 +1425,8 @@
         in_specs=[
             pl.BlockSpec((960, 128), lambda i: (i, 0)),
             pl.BlockSpec((960, 128), lambda i: (5 + i, 0)),
-            pl.BlockSpec((960, 128), lambda i: (10 + i, 0)),
-            pl.BlockSpec((480, 128), lambda i: (30 + jnp.minimum(i, 3), 0)),
+            pl.BlockSpec((960, 128), lambda i: (12 + i, 0)),
+            pl.BlockSpec((480, 128), lambda i: (20 + jnp.minimum(i, 3), 0)),
             whole(*qkv.shape),
         ],
         out_specs=[
@@ -1351,10 +1487,12 @@
     ready = Reduction(
         (
             (nb_t.reshape(2, 2, 240, 128), dgu),
+            (at_t.reshape(2, 2, 240, 128), branch),
             (cot_t, hidden.reshape(2, 2, TOK, 640)),
-            (at_t.reshape(2, 2, 240, 128), branch),
         ),
         None,
+        False,
+        192,
     )
     dq_rows, dkv, done = backward(q_rows, do_rows, o_rows, logs, kv, own_kv, plan, ready, 2)
     grad_tokens, grad_qkv, grad_gain_a = unproject(
@@ -1364,7 +1502,7 @@
     gain_rows = jnp.pad(gain_rows, ((0, 0), (0, 0), (0, 16))).reshape(2, 2, 4, 128).astype(BF16)
     gain_rows = jnp.pad(gain_rows, ((0, 0), (0, 0), (0, 12), (0, 0)))
     late = Reduction(((na_t.reshape(2, 2, 240, 128), grad_qkv),), gain_rows, True)
-    flat_done, flat = finish(done, ready.sizes, ready.used, late, 3)
+    flat_done, flat = finish(done, ready, late, 3)
     shard_g, shard_u, shard_d, shard_o, shard_q, shard_k, shard_v = unpack(flat_done, flat)
     shard_gains = flat[3120:3124].reshape(2, 256)[:, :240].astype(F32)
     return (

time: 296 us -> 287 us (0.970)
  Pallas kernels: 267 us -> 258 us
    pallas_call x1, Pallas kernels: 104 us -> 91.9 us  [backward(): pl.pallas_call(functools.partial(backward_kernel, reduction), out_shape=[...]
    pallas_call x1, Pallas kernels: 47.9 us -> 53 us  [finish(): pl.pallas_call(functools.partial(finish_kernel, reduction, ready.sizes, r...]
where the time goes in v2:
time: 287 us; the launch traced here: 285 us
  Pallas kernels  258 us (90%)
  local copies, waits for them, and re-layouts  18.2 us (6%)
  other arithmetic  5.67 us (2%)
    pallas_call x1, Pallas kernels, backward(): pl.pallas_call(functools.partial(backward_kernel, reduction), out_shape=[...  91.9 us
    pallas_call x1, Pallas kernels, forward(): pl.pallas_call(functools.partial(forward_kernel, n), out_shape=[jax.Shape...  63 us
    pallas_call x1, Pallas kernels, finish(): pl.pallas_call(functools.partial(finish_kernel, reduction, ready.sizes, r...  53 us
    pallas_call x1, Pallas kernels, gather_weights(): pl.pallas_call(functools.partial(gather_kernel, n), out_shape=gathered(ar...  18.1 us
    pallas_call x1, Pallas kernels, middle(): pl.pallas_call(middle_kernel, out_shape=[jax.ShapeDtypeStruct((TOK, D), B...  14.4 us
    unnamed x16, local copies, waits for them, and re-layouts  9.88 us
    pallas_call x1, Pallas kernels, unpack(): pl.pallas_call(unpack_kernel, grid=(5,), out_shape=[jax.ShapeDtypeStruct(...  8.16 us

profile of v2, /device:TPU:1, one launch (start us, length us, event | category | flops | bytes accessed | tf_op | source)
XLA Modules:
  0.0 284.9 jit_solution(18397748568894934898)
XLA Ops:
  0.6 0.0 copy-start.2
  0.7 1.4 fusion.10
  2.7 0.6 fusion.15
  4.6 0.7 fusion.9
  5.3 0.7 stack.18
  5.9 0.7 stack.19
  6.6 0.6 fusion.8.refs_0_
  7.2 1.0 sine_multiply_fusion
  8.2 1.1 copy.26
  9.3 1.1 copy.27
  10.4 1.1 copy.23
  11.5 1.1 copy.29
  12.6 1.0 maximum_select_fusion.1
  13.6 0.0 copy-done.2
  13.7 1.1 concatenate.18.refs_1_
  14.8 18.1 %gather_weights.1 = (bf16[64,256]{1,0:T(8,128)(2,1)}, bf16[960,1664]{1,0:T(8,128)(2,1)}) custom-call(bf16[16,256]{1,0:T(8,128)(2,1)} %fusion.8.refs_0_, bf16[240,1664]{1,0:T(8,128)(2,1)} %concatenate.18.refs_1_), custom_call_target="tpu_custom_call" | custom-call | tf_op jit(solution)/shard_map/gather_weights/pallas_call | solution.py:147
  32.9 0.7 slice.86
  33.6 0.7 reshape_squeeze.7.gain
  34.3 0.7 reshape_squeeze.6.gain
  35.0 4.6 %project.1 = (bf16[5,192,128]{2,1,0:T(8,128)(2,1)}, bf16[640,128]{1,0:T(8,128)(2,1)}, bf16[960,128]{1,0:T(8,128)(2,1)}, f32[33,128]{1,0:T(8,128)}, f32[33,128]{1...) custom-call(s32[64]{0:T(128)} %table.1, bf16[128,960]{1,0:T(8,128)(2,1)} %get-tuple-element.122.tok, ...), custom_call_target="tpu_custom_call" | custom-call | tf_op jit(solution)/shard_map/project/pallas_call | solution.py:1258
  39.5 63.0 %forward.1 = (f32[5,192,128]{2,1,0:T(8,128)}, f32[5,192,128]{2,1,0:T(8,128)}, bf16[4,2,4,640,128]{4,3,2,1,0:T(8,128)(2,1)}, bf16[960,960]{1,0:T(8,128)(2,1)}, bf...) custom-call(bf16[5,192,128]{2,1,0:T(8,128)(2,1)} %get-tuple-element.54.q_ref.refs_0_, ...), custom_call_target="tpu_custom_call" | custom-call | tf_op jit(solution)/shard_map/forward/pallas_call | solution.py:509
  102.5 14.4 %middle.1 = (bf16[128,960]{1,0:T(8,128)(2,1)}, f32[128,960]{1,0:T(8,128)}, bf16[5,192,128]{2,1,0:T(8,128)(2,1)}, f32[1,960]{1,0:T(1,128)}, bf16[960,128]{1,0:T(8...) custom-call(f32[5,192,128]{2,1,0:T(8,128)} %get-tuple-element.59.o.r, ...), custom_call_target="tpu_custom_call" | custom-call | tf_op jit(solution)/shard_map/middle/pallas_call | solution.py:1326
  117.0 91.9 %backward.1 = (f32[5,192,128]{2,1,0:T(8,128)}, f32[640,128]{1,0:T(8,128)}, bf16[832,128]{1,0:T(8,128)(2,1)}) custom-call(bf16[5,192,128]{2,1,0:T(8,128)(2,1)} %get-tuple-element.54.q_ref.refs_0_, bf16[5,192,128]{2,1,0:T(8,128)(2,1)} %get-tuple-element.65.refs_1_, f32[5,192,128]{2,1,0:T(8,128)} %get-tuple-element.59.o.refs_2_, ...), custom_call_target="tpu_custom_call" | custom-call | tf_op jit(solution)/shard_map/backward/pallas_call | solution.py:1058
  208.9 0.0 copy-start.3
  208.9 0.0 copy-start.1
  208.9 5.1 %unproject.1 = (f32[128,960]{1,0:T(8,128)}, bf16[1,128,1664]{2,1,0:T(8,128)(2,1)}, f32[1,960]{1,0:T(1,128)}) custom-call(f32[5,192,128]{2,1,0:T(8,128)} %get-tuple-element.75.dq, f32[640,128]{1,0:T(8,128)} %get-tuple-element.76.dkv, f32[128,128]{1,0:T(8,128)} %get-tuple-element.117.cosine, f32[128,128]{1,0:T(8,128)} %get-tuple-element.116.sine, ...), custom_call_target="tpu_custom_call" | custom-call | tf_op jit(solution)/shard_map/unproject/pallas_call | solution.py:1369
  214.0 0.0 copy-start
  214.0 0.8 convert_reduce_fusion.1
  214.8 0.1 stack.24
  214.9 0.0 copy-done.3
  214.9 0.1 stack.25
  215.1 0.6 pad.15.refs_3_
  215.7 0.0 copy-done.1
  215.7 0.1 fusion.1
  215.8 0.8 copy.34
  216.6 1.1 fusion.11
  217.7 0.0 copy-done
  217.7 0.1 fusion
  217.8 1.0 copy.35
  218.8 53.0 %finish.1 = (bf16[16384,128]{1,0:T(8,128)(2,1)}, bf16[3328,128]{1,0:T(8,128)(2,1)}) custom-call(bf16[832,128]{1,0:T(8,128)(2,1)} %get-tuple-element.79.refs_0_, bf16[2,2,240,128]{3,2,1,0:T(8,128)(2,1)} %bitcast.36, bf16[1,128,1664]{2,1,0:T(8,128)(2,1)} %get-tuple-element.81.refs_2_, bf16[2,2,16,128]{3,2,1,0:T(8,128)(2,1)} %pad.15.refs_3_), custom_call_target="tpu_custom_call" | custom-call | tf_op jit(solution)/shard_map/finish/pallas_call | solution.py:1127
  271.7 0.7 slice.80
  272.4 0.6 fusion.14
  273.0 8.2 %unpack.1 = (f32[240,2560]{1,0:T(8,128)}, f32[240,2560]{1,0:T(8,128)}, f32[960,640]{1,0:T(8,128)}, f32[240,960]{1,0:T(8,128)}, f32[240,960]{1,0:T(8,128)}, /*index=5*/f32[240,320]{1,0:T(8,128)}, f32[240,320]{1,0:T(8,128)}) custom-call(bf16[16384,128]{1,0:T(8,128)(2,1)} %get-tuple-element.85.g_in.u_in.d_in.o_in, ...), custom_call_target="tpu_custom_call" | custom-call | tf_op jit(solution)/shard_map/unpack/pallas_call | solution.py:1416
  281.2 1.9 copy.36
  283.0 1.9 copy.37
  (15 shorter events, 0.2 us)
Async XLA Ops:
  0.6 13.0 %copy-start.2 = (bf16[240,960]{1,0:T(8,128)(2,1)S(1)}, bf16[240,960]{1,0:T(8,128)(2,1)}, u32[]{:S(2)}) copy-start(bf16[240,960]{1,0:T(8,128)(2,1)} %param.16) | copy-start | bytes 1382404
  208.9 6.0 %copy-start.3 = (f32[1,960]{1,0:T(1,128)S(1)}, f32[1,960]{1,0:T(1,128)}, u32[]{:S(2)}) copy-start(f32[1,960]{1,0:T(1,128)} %get-tuple-element.83) | copy-start | bytes 11524
  208.9 6.8 %copy-start.1 = (bf16[128,960]{1,0:T(8,128)(2,1)S(1)}, bf16[128,960]{1,0:T(8,128)(2,1)}, u32[]{:S(2)}) copy-start(bf16[128,960]{1,0:T(8,128)(2,1)} %get-tuple-element.64) | copy-start | bytes 737284
  214.0 3.7 %copy-start = (f32[128,960]{1,0:T(8,128)S(1)}, f32[128,960]{1,0:T(8,128)}, u32[]{:S(2)}) copy-start(f32[128,960]{1,0:T(8,128)} %get-tuple-element.78) | copy-start | bytes 1474564

commit v3 on v2

--- a/solution.py
+++ b/solution.py
@@ -3,6 +3,7 @@
 
 import jax
 import jax.numpy as jnp
+import numpy as np
 from jax import lax
 from jax.experimental import pallas as pl
 from jax.experimental.pallas import tpu as pltpu
@@ -126,39 +127,46 @@
         copy.wait_send()
 
 
-def gather_kernel(count, *refs):
-    arrays = list(zip(refs[:count], refs[count : 2 * count]))
-    send, recv, local = refs[2 * count :]
+def gathered(arrays):
+    return [jax.ShapeDtypeStruct((4 * a.shape[0], *a.shape[1:]), a.dtype) for a in arrays]
+
+
+def gather_qkv_kernel(
+    gain_a, gain_b, wq, wk_t, wv_t, gains, qkv, gains_own, qkv_own, send, recv, local
+):
+    blank = jnp.zeros((1, 16), F32)
+    lines = [jnp.concatenate([g[...].astype(F32), blank], axis=1) for g in (gain_a, gain_b)]
+    gains_own[...] = jnp.concatenate([*lines, jnp.zeros((14, 256), F32)], axis=0).astype(BF16)
+    qkv_own[:, 0:896] = wq[:, 0:896]
+    rest = [wq[:, 896:960].astype(F32), wk_t[...].astype(F32).T, wv_t[...].astype(F32).T]
+    qkv_own[:, 896:1664] = jnp.concatenate([*rest, jnp.zeros((240, 64), F32)], axis=1).astype(BF16)
     me = here()
     flip = 1 - me["yl"]
     greet((device(me, yl=flip), device(me, yl=flip, yh=1 - me["yh"]), device(me, c=1 - me["c"])))
     sems = Sems(send, recv)
-    started = start_gather(me, sems, local, arrays)
+    started = start_gather(me, sems, local, [(gains_own, gains), (qkv_own, qkv)])
     relay_gather(me, sems, started)
     end_gather(started)
 
 
-def gathered(arrays):
-    return [jax.ShapeDtypeStruct((4 * a.shape[0], *a.shape[1:]), a.dtype) for a in arrays]
-
-
-def gather_weights(arrays, collective_id):
-    n = len(arrays)
+def gather_qkv(gain_a, gain_b, wq, wk_t, wv_t, collective_id):
+    own = [jax.ShapeDtypeStruct((16, 256), BF16), jax.ShapeDtypeStruct((240, 1664), BF16)]
     return pl.pallas_call(
-        functools.partial(gather_kernel, n),
-        out_shape=gathered(arrays),
-        in_specs=[VM] * n,
-        out_specs=[ANY] * n,
-        scratch_shapes=[
-            pltpu.SemaphoreType.DMA((5 * n,)),
-            pltpu.SemaphoreType.DMA((5 * n,)),
-            pltpu.SemaphoreType.DMA((n,)),
+        gather_qkv_kernel,
+        out_shape=gathered(own),
+        in_specs=[VM] * 5,
+        out_specs=[ANY] * 2,
+        scratch_shapes=[pltpu.VMEM(a.shape, BF16) for a in own]
+        + [
+            pltpu.SemaphoreType.DMA((10,)),
+            pltpu.SemaphoreType.DMA((10,)),
+            pltpu.SemaphoreType.DMA((2,)),
         ],
         compiler_params=pltpu.CompilerParams(
             collective_id=collective_id, has_side_effects=True, vmem_limit_bytes=BIG
         ),
-        name="gather_weights",
-    )(*arrays)
+        name="gather_qkv",
+    )(gain_a, gain_b, wq, wk_t, wv_t)
 
 
 class Ring:
@@ -1208,14 +1216,40 @@
     return grad_values, jnp.sum(grad * values * inv, axis=0, keepdims=True)
 
 
+def swapped(table):
+    ctx = lax.axis_index("ctx")
+    return jnp.where(table[2 * ctx] > table[2 * ctx + 1], 1.0, 0.0)
+
+
+def swap_lanes(a, swap):
+    return a * (1.0 - swap) + turn(a) * swap
+
+
 def project_kernel(
-    table, tok, gain, w, cosine, sine, q_ref, own_ref, nt_ref, flag, left, right, limit
+    table, tok_t, cot_t, gains, w, frequency,
+    q_ref, own_ref, nt_ref, tok_ref, cot_ref, cott_ref, cosine, sine, gain_a, gain_b,
+    flag, left, right, limit,
 ):
-    values = tok[...].astype(F32)
-    normed = values * inverse_rms(values) * gain[...]
+    ctx = lax.axis_index("ctx")
+    mine = jnp.minimum(table[2 * ctx], table[2 * ctx + 1])
+    swap = swapped(table)
+    for row, ref in enumerate((gain_a, gain_b)):
+        parts = [gains[16 * f : 16 * (f + 1), :].astype(F32)[row : row + 1, :240] for f in range(4)]
+        ref[...] = jnp.concatenate(parts, axis=1)
+    line = lax.broadcasted_iota(jnp.int32, (TOK, 128), 0)
+    column = lax.broadcasted_iota(jnp.int32, (TOK, 128), 1)
+    position = jnp.where(line < HALF, mine, 63 - mine) * HALF + lax.rem(line, HALF)
+    angles = position.astype(F32) * frequency[...]
+    cosine[...] = jnp.cos(angles)
+    sine[...] = jnp.where(column % HEAD < 32, -1.0, 1.0) * jnp.sin(angles)
+    cot = swap_lanes(cot_t[...].astype(F32), swap)
+    cott_ref[0] = cot.astype(BF16)
+    cot_ref[...] = cot.T.astype(BF16)
+    values = swap_lanes(tok_t[...].astype(F32), swap).T
+    tok_ref[...] = values.astype(BF16)
+    normed = values * inverse_rms(values) * gain_a[...]
     low = normed.astype(BF16)
     nt_ref[...] = normed.T.astype(BF16)
-    lanes = low_lanes(HALF)
     blocks = []
     for t in range(13):
         u = dot_nn(low, w[:, t * 128 : (t + 1) * 128])
@@ -1228,8 +1262,6 @@
     for i in range(2 * KV_HEADS):
         own_ref[i * HALF : (i + 1) * HALF, :] = turn(blocks[HEADS + i]).astype(BF16)
 
-    ctx = lax.axis_index("ctx")
-    mine = jnp.minimum(table[2 * ctx], table[2 * ctx + 1])
     lane = lax.broadcasted_iota(jnp.int32, (1, 128), 1)
     first = lane < HALF
     offset = lax.rem(lane, HALF)
@@ -1254,25 +1286,37 @@
     limit[CTX:TILES, :] = jnp.where(first, offset, 10**6).astype(F32)
 
 
-def project(table, tok, gain, w, cosine, sine):
+SMEM = pl.BlockSpec(memory_space=pltpu.SMEM)
+
+
+def project(table, tok_t, cot_t, gains, w):
+    exponent = -(np.arange(128) % 32).astype(np.float32) / 32
+    frequency = jnp.asarray(np.power(BASE, exponent).astype(np.float32).reshape(1, 128))
     return pl.pallas_call(
         project_kernel,
         out_shape=[
             jax.ShapeDtypeStruct((KV_HEADS, ROWS, 128), BF16),
             jax.ShapeDtypeStruct((640, 128), BF16),
             jax.ShapeDtypeStruct((D, 128), BF16),
+            jax.ShapeDtypeStruct((TOK, D), BF16),
+            jax.ShapeDtypeStruct((TOK, D), BF16),
+            jax.ShapeDtypeStruct((1, D, 128), BF16),
+            jax.ShapeDtypeStruct((TOK, 128), F32),
+            jax.ShapeDtypeStruct((TOK, 128), F32),
+            jax.ShapeDtypeStruct((1, D), F32),
+            jax.ShapeDtypeStruct((1, D), F32),
         ]
         + [jax.ShapeDtypeStruct((TILES, 128), F32)] * 4,
-        in_specs=[pl.BlockSpec(memory_space=pltpu.SMEM)] + [VM] * 5,
-        out_specs=[VM] * 7,
+        in_specs=[SMEM] + [VM] * 5,
+        out_specs=[VM] * 14,
         compiler_params=pltpu.CompilerParams(vmem_limit_bytes=BIG),
         name="project",
-    )(table, tok, gain, w, cosine, sine)
+    )(table, tok_t, cot_t, gains, w, frequency)
 
 
 def middle_kernel(
-    o, tok, cot, gain, out_hbm, gate_hbm, up_hbm, down_hbm,
-    layer_out, grad_mid, do_rows, gain_grad, nt, dgu, gt, hid, at_t, gb,
+    table, o, tok, cot, gain, out_hbm, gate_hbm, up_hbm, down_hbm,
+    layer_out, grad_mid, do_rows, gain_grad, nt, dgu, hid, at_t, gb,
     out_w, gate_w, up_w, down_w, sem,
 ):
     loads = []
@@ -1284,7 +1328,6 @@
     attended = jnp.concatenate(get_heads(o), axis=1)
     at_t[...] = attended.T[:D].astype(BF16)
     cot_low = cot[...]
-    gt[0] = cot_low.astype(F32).T.astype(BF16)
     loads[0].wait()
     middle = tok[...].astype(F32) + dot_nn(attended.astype(BF16)[:, :D], out_w[...])
     inv = inverse_rms(middle)
@@ -1304,7 +1347,7 @@
     total = middle
     for f in range(4):
         total = total + dot_nt(hidden[:, f * 640 : (f + 1) * 640], down_w[f * D : (f + 1) * D, :])
-    layer_out[...] = total.astype(BF16)
+    layer_out[...] = swap_lanes(total.T, swapped(table)).astype(BF16)
     grad_hidden = jnp.concatenate(
         [dot_nn(cot_low, down_w[f * D : (f + 1) * D, :]) for f in range(4)], axis=1
     )
@@ -1321,32 +1364,33 @@
     put_heads(do_rows, dot_nt(branch, out_w[...]))
 
 
-def middle(o, tok, cot, gain, out_w, gate_w, up_w, down_w):
+def middle(table, o, tok, cot, gain, out_w, gate_w, up_w, down_w):
     weights = (out_w, gate_w, up_w, down_w)
     return pl.pallas_call(
         middle_kernel,
         out_shape=[
-            jax.ShapeDtypeStruct((TOK, D), BF16),
+            jax.ShapeDtypeStruct((D, TOK), BF16),
             jax.ShapeDtypeStruct((TOK, D), F32),
             jax.ShapeDtypeStruct((KV_HEADS, ROWS, 128), BF16),
             jax.ShapeDtypeStruct((1, D), F32),
             jax.ShapeDtypeStruct((D, 128), BF16),
             jax.ShapeDtypeStruct((1, TOK, 2 * FF), BF16),
-            jax.ShapeDtypeStruct((1, D, 128), BF16),
             jax.ShapeDtypeStruct((4, TOK, 640), BF16),
             jax.ShapeDtypeStruct((D, 128), BF16),
             jax.ShapeDtypeStruct((1, TOK, 1024), BF16),
         ],
-        in_specs=[VM] * 4 + [ANY] * 4,
-        out_specs=[VM] * 10,
+        in_specs=[SMEM] + [VM] * 4 + [ANY] * 4,
+        out_specs=[VM] * 9,
         scratch_shapes=[pltpu.VMEM(w.shape, BF16) for w in weights]
         + [pltpu.SemaphoreType.DMA((4,))],
         compiler_params=pltpu.CompilerParams(vmem_limit_bytes=BIG),
         name="middle",
-    )(o, tok, cot, gain, *weights)
-
-
-def unproject_kernel(dq, dkv, cosine, sine, w, tok, gain, grad_mid, grad_tok, dqkv, gain_grad):
+    )(table, o, tok, cot, gain, *weights)
+
+
+def unproject_kernel(
+    table, dq, dkv, cosine, sine, w, tok, gain, grad_mid, gain_grad_b, grad_tok, dqkv, gain_rows
+):
     tiles = get_heads(dq)
     low = low_lanes(TOK)
     turned = [turn(dkv[i * 128 : (i + 1) * 128, :].T) for i in range(5)]
@@ -1361,26 +1405,33 @@
         dqkv[0, :, t * 128 : (t + 1) * 128] = u.astype(BF16)
     grad_norm = dot_nt(dqkv[0], w[...])
     values = tok[...].astype(F32)
-    grad_values, gain_grad[...] = norm_back(values, inverse_rms(values), gain[...], grad_norm)
-    grad_tok[...] = grad_mid[...] + grad_values
-
-
-def unproject(dq, dkv, cosine, sine, w, tok, gain, grad_mid):
+    grad_values, gain_grad = norm_back(values, inverse_rms(values), gain[...], grad_norm)
+    grad_tok[...] = swap_lanes((grad_mid[...] + grad_values).T, swapped(table))
+    blank, below = jnp.zeros((1, 16), F32), jnp.zeros((12, 128), F32)
+    for f in range(4):
+        lines = []
+        for grad in (gain_grad, gain_grad_b[...]):
+            both = jnp.concatenate([grad[:, f * 240 : (f + 1) * 240], blank], axis=1)
+            lines += [both[:, :128], both[:, 128:]]
+        gain_rows[f] = jnp.concatenate([*lines, below], axis=0).astype(BF16)
+
+
+def unproject(table, dq, dkv, cosine, sine, w, tok, gain, grad_mid, gain_grad_b):
     return pl.pallas_call(
         unproject_kernel,
         out_shape=[
-            jax.ShapeDtypeStruct((TOK, D), F32),
+            jax.ShapeDtypeStruct((D, TOK), F32),
             jax.ShapeDtypeStruct((1, TOK, 1664), BF16),
-            jax.ShapeDtypeStruct((1, D), F32),
+            jax.ShapeDtypeStruct((4, 16, 128), BF16),
         ],
-        in_specs=[VM] * 8,
+        in_specs=[SMEM] + [VM] * 9,
         out_specs=[VM] * 3,
         compiler_params=pltpu.CompilerParams(vmem_limit_bytes=BIG),
         name="unproject",
-    )(dq, dkv, cosine, sine, w, tok, gain, grad_mid)
-
-
-def unpack_kernel(g_in, u_in, d_in, o_in, qkv, g, u, d, o, q, k, v):
+    )(table, dq, dkv, cosine, sine, w, tok, gain, grad_mid, gain_grad_b)
+
+
+def unpack_kernel(g_in, u_in, d_in, o_in, qkv, g, u, d, o, q, k, v, gain_a, gain_b):
     for t in range(4):
         rows, lanes = slice(t * 240, (t + 1) * 240), slice(t * 128, (t + 1) * 128)
         g[:, lanes] = g_in[rows, :].astype(F32)
@@ -1401,12 +1452,16 @@
             q[:, t * 128 : (t + 1) * 128] = tiles[t]
         q[:, 896:960] = tiles[7][:, :64]
         turned = [turn(t) for t in tiles[7:10]]
-        k[:, 0:128] = jnp.where(low, turned[0], turned[1])
-        k[:, 128:256] = jnp.where(low, turned[1], turned[2])
-        k[:, 256:320] = turned[2][:, :64]
-        v[:, 0:128] = tiles[10]
-        v[:, 128:256] = tiles[11]
-        v[:, 256:320] = tiles[12][:, :64]
+        k[0:128, :] = jnp.where(low, turned[0], turned[1]).T
+        k[128:256, :] = jnp.where(low, turned[1], turned[2]).T
+        k[256:320, :] = turned[2].T[:64]
+        v[0:128, :] = tiles[10].T
+        v[128:256, :] = tiles[11].T
+        v[256:320, :] = tiles[12].T[:64]
+        lines = qkv[3120:3136, :].astype(F32)
+        for n, ref in enumerate((gain_a, gain_b)):
+            both = [lines[2 * n : 2 * n + 1], lines[2 * n + 1 : 2 * n + 2, :112]]
+            ref[...] = jnp.concatenate(both, axis=1)
 
 
 def unpack(done, qkv):
@@ -1419,7 +1474,8 @@
         out_shape=[
             jax.ShapeDtypeStruct(shape, F32)
             for shape in (
-                (240, FF), (240, FF), (D, 640), (240, D), (240, D), (240, 320), (240, 320),
+                (240, FF), (240, FF), (D, 640), (240, D), (240, D), (320, 240), (320, 240),
+                (1, 240), (1, 240),
             )
         ],
         in_specs=[
@@ -1435,54 +1491,32 @@
             pl.BlockSpec((D, 128), lambda i: (0, i)),
             pl.BlockSpec((240, 256), lambda i: (0, jnp.minimum(i, 3))),
             whole(240, D),
-            whole(240, 320),
-            whole(240, 320),
+            whole(320, 240),
+            whole(320, 240),
+            whole(1, 240),
+            whole(1, 240),
         ],
         compiler_params=pltpu.CompilerParams(vmem_limit_bytes=BIG),
         name="unpack",
     )(done, done, done, done, qkv)
 
 
-def rope_tables(early):
-    row = lax.broadcasted_iota(jnp.int32, (TOK, 128), 0)
-    lane = lax.broadcasted_iota(jnp.int32, (TOK, 128), 1)
-    block = jnp.where(row < HALF, early, 63 - early)
-    position = (block * HALF + row % HALF).astype(F32)
-    frequency = BASE ** (-(lane % 32).astype(F32) / 32)
-    angles = position * frequency
-    return jnp.cos(angles), jnp.where(lane % HEAD < 32, -1.0, 1.0) * jnp.sin(angles)
-
-
-def swap_rows(a, swap):
-    return jnp.where(swap, jnp.concatenate([a[HALF:], a[:HALF]], axis=0), a)
-
-
 def on_device(
     tokens, cotangent, block_table, attn_gain, w_query, w_key, w_value, w_out, mlp_gain,
     w_gate, w_up, w_down,
 ):
-    ctx = lax.axis_index("ctx")
-    gains = jnp.pad(jnp.stack([attn_gain, mlp_gain]), ((0, 14), (0, 16)))
-    blank = jnp.zeros((240, 64), BF16)
-    qkv_shard = jnp.concatenate([w_query, w_key, w_value, blank], axis=1)
-    gains_all, qkv_w = gather_weights((gains, qkv_shard), 0)
-    gains_all = gains_all.reshape(4, 16, 256)[:, :2, :240].astype(F32)
-    gain_a = gains_all[:, 0].reshape(1, D)
-    gain_b = gains_all[:, 1].reshape(1, D)
-
-    own_blocks = lax.dynamic_slice_in_dim(block_table, 2 * ctx, 2)
-    swap = own_blocks[0] > own_blocks[1]
-    cosine, sine = rope_tables(jnp.min(own_blocks))
-    tok = swap_rows(tokens[0], swap)
-    cot = swap_rows(cotangent[0], swap)
-
-    q_rows, own_kv, na_t, *plan = project(block_table, tok, gain_a, qkv_w, cosine, sine)
+    gains, qkv_w = gather_qkv(
+        attn_gain.reshape(1, 240), mlp_gain.reshape(1, 240), w_query, w_key.T, w_value.T, 0
+    )
+    q_rows, own_kv, na_t, tok, cot, cot_t, cosine, sine, gain_a, gain_b, *plan = project(
+        block_table, tokens[0].T, cotangent[0].T, gains, qkv_w
+    )
     o_rows, logs, kv, out_w, gate_w, up_w, down_w = forward(
         q_rows, own_kv, plan, (w_out, w_gate, w_up, w_down.T), 1
     )
     kv = kv.reshape(CTX, 640, 128)
-    layer_out, grad_mid, do_rows, grad_gain_b, nb_t, dgu, cot_t, hidden, at_t, branch = middle(
-        o_rows, tok, cot, gain_b, out_w, gate_w, up_w, down_w
+    layer_out, grad_mid, do_rows, grad_gain_b, nb_t, dgu, hidden, at_t, branch = middle(
+        block_table, o_rows, tok, cot, gain_b, out_w, gate_w, up_w, down_w
     )
     ready = Reduction(
         (
@@ -1495,25 +1529,25 @@
         192,
     )
     dq_rows, dkv, done = backward(q_rows, do_rows, o_rows, logs, kv, own_kv, plan, ready, 2)
-    grad_tokens, grad_qkv, grad_gain_a = unproject(
-        dq_rows, dkv, cosine, sine, qkv_w, tok, gain_a, grad_mid
-    )
-    gain_rows = jnp.stack([grad_gain_a, grad_gain_b]).reshape(2, 4, 240).transpose(1, 0, 2)
-    gain_rows = jnp.pad(gain_rows, ((0, 0), (0, 0), (0, 16))).reshape(2, 2, 4, 128).astype(BF16)
-    gain_rows = jnp.pad(gain_rows, ((0, 0), (0, 0), (0, 12), (0, 0)))
-    late = Reduction(((na_t.reshape(2, 2, 240, 128), grad_qkv),), gain_rows, True)
+    grad_tokens, grad_qkv, gain_rows = unproject(
+        block_table, dq_rows, dkv, cosine, sine, qkv_w, tok, gain_a, grad_mid, grad_gain_b
+    )
+    late = Reduction(
+        ((na_t.reshape(2, 2, 240, 128), grad_qkv),), gain_rows.reshape(2, 2, 16, 128), True
+    )
     flat_done, flat = finish(done, ready, late, 3)
-    shard_g, shard_u, shard_d, shard_o, shard_q, shard_k, shard_v = unpack(flat_done, flat)
-    shard_gains = flat[3120:3124].reshape(2, 256)[:, :240].astype(F32)
+    shard_g, shard_u, shard_d, shard_o, shard_q, shard_k, shard_v, total_a, total_b = unpack(
+        flat_done, flat
+    )
     return (
-        swap_rows(layer_out, swap)[None],
-        swap_rows(grad_tokens, swap)[None],
-        shard_gains[0],
+        layer_out.T[None],
+        grad_tokens.T[None],
+        total_a.reshape(240),
         shard_q,
-        shard_k,
-        shard_v,
+        shard_k.T,
+        shard_v.T,
         shard_o,
-        shard_gains[1],
+        total_b.reshape(240),
         shard_g,
         shard_u,
         shard_d.T,

time: 287 us -> 266 us (0.927)
  local copies, waits for them, and re-layouts: 18.2 us -> 2.44 us
  other arithmetic: 5.67 us -> 0 us
    unnamed x16 -> x0, local copies, waits for them, and re-layouts: 9.88 us -> none
    slice x9 -> x0, local copies, waits for them, and re-layouts: 3.69 us -> none  [the longest x4 1.13 us: swap_rows(): return jnp.where(swap, jnp.concatenate([a[HALF:], a[:HALF]], axis=0), a)]
where the time goes in v3:
time: 266 us; the launch traced here: 264 us
  Pallas kernels  260 us (98%)
    pallas_call x1, Pallas kernels, backward(): pl.pallas_call(functools.partial(backward_kernel, reduction), out_shape=[...  92 us
    pallas_call x1, Pallas kernels, forward(): pl.pallas_call(functools.partial(forward_kernel, n), out_shape=[jax.Shape...  63 us
    pallas_call x1, Pallas kernels, finish(): pl.pallas_call(functools.partial(finish_kernel, reduction, ready.sizes, r...  53.2 us
    pallas_call x1, Pallas kernels, gather_qkv(): pl.pallas_call(gather_qkv_kernel, out_shape=gathered(own), in_specs=[VM]...  18.4 us
    pallas_call x1, Pallas kernels, middle(): pl.pallas_call(middle_kernel, out_shape=[jax.ShapeDtypeStruct((D, TOK), B...  14.5 us
    pallas_call x1, Pallas kernels, unpack(): pl.pallas_call(unpack_kernel, grid=(5,), out_shape=[jax.ShapeDtypeStruct(...  8.36 us
    pallas_call x1, Pallas kernels, project(): pl.pallas_call(project_kernel, out_shape=[jax.ShapeDtypeStruct((KV_HEADS,...  5.57 us
    pallas_call x1, Pallas kernels, unproject(): pl.pallas_call(unproject_kernel, out_shape=[jax.ShapeDtypeStruct((D, TOK)...  5.46 us

profile of v3, /device:TPU:1, one launch (start us, length us, event | category | flops | bytes accessed | tf_op | source)
XLA Modules:
  0.0 263.8 jit_solution(13269486640512387279)
XLA Ops:
  0.6 1.2 reshape.52.gain_a
  1.9 1.2 reshape.53.gain_b
  3.1 18.4 %gather_qkv.1 = (bf16[64,256]{1,0:T(8,128)(2,1)}, bf16[960,1664]{1,0:T(8,128)(2,1)}) custom-call(bf16[1,240]{1,0:T(2,128)(2,1)} %reshape.52.gain_a, bf16[1,240]{1,0:T(2,128)(2,1)} %reshape.53.gain_b, bf16[240,960]{1,0:T(8,128)(2,1)} %wq.1, bf16[320,240]{1,0:T(8,128)(2,1)} %bitcast.34, bf16[320,240]{1,0:T(8,128)(2,1)} %bitcast.35), custom_call_target="tpu_custom_call" | custom-call | tf_op jit(solution)/shard_map/gather_qkv/pallas_call | solution.py:154
  21.5 5.6 %project.1 = (bf16[5,192,128]{2,1,0:T(8,128)(2,1)}, bf16[640,128]{1,0:T(8,128)(2,1)}, bf16[960,128]{1,0:T(8,128)(2,1)}, bf16[128,960]{1,0:T(8,128)(2,1)}, bf16[1...) custom-call(s32[64]{0:T(128)} %table.5, ...), custom_call_target="tpu_custom_call" | custom-call | tf_op jit(solution)/shard_map/project/pallas_call | solution.py:1295
  27.0 63.0 %forward.1 = (f32[5,192,128]{2,1,0:T(8,128)}, f32[5,192,128]{2,1,0:T(8,128)}, bf16[4,2,4,640,128]{4,3,2,1,0:T(8,128)(2,1)}, bf16[960,960]{1,0:T(8,128)(2,1)}, bf...) custom-call(bf16[5,192,128]{2,1,0:T(8,128)(2,1)} %get-tuple-element.62.q_ref.refs_0_, ...), custom_call_target="tpu_custom_call" | custom-call | tf_op jit(solution)/shard_map/forward/pallas_call | solution.py:517
  90.0 14.5 %middle.1 = (bf16[960,128]{1,0:T(8,128)(2,1)}, f32[128,960]{1,0:T(8,128)}, bf16[5,192,128]{2,1,0:T(8,128)(2,1)}, f32[1,960]{1,0:T(1,128)}, bf16[960,128]{1,0:T(8...) custom-call(s32[64]{0:T(128)} %table.5, ...), custom_call_target="tpu_custom_call" | custom-call | tf_op jit(solution)/shard_map/middle/pallas_call | solution.py:1369
  104.5 92.0 %backward.1 = (f32[5,192,128]{2,1,0:T(8,128)}, f32[640,128]{1,0:T(8,128)}, bf16[832,128]{1,0:T(8,128)(2,1)}) custom-call(bf16[5,192,128]{2,1,0:T(8,128)(2,1)} %get-tuple-element.62.q_ref.refs_0_, bf16[5,192,128]{2,1,0:T(8,128)(2,1)} %get-tuple-element.76.refs_1_, f32[5,192,128]{2,1,0:T(8,128)} %get-tuple-element.67.o.refs_2_, ...), custom_call_target="tpu_custom_call" | custom-call | tf_op jit(solution)/shard_map/backward/pallas_call | solution.py:1066
  196.5 5.5 %unproject.1 = (f32[960,128]{1,0:T(8,128)}, bf16[1,128,1664]{2,1,0:T(8,128)(2,1)}, bf16[4,16,128]{2,1,0:T(8,128)(2,1)}) custom-call(s32[64]{0:T(128)} %table.5, f32[5,192,128]{2,1,0:T(8,128)} %get-tuple-element.86.dq, f32[640,128]{1,0:T(8,128)} %get-tuple-element.87.dkv, f32[128,128]{1,0:T(8,128)} %get-tuple-element.88.cosine, ...), custom_call_target="tpu_custom_call" | custom-call | tf_op jit(solution)/shard_map/unproject/pallas_call | solution.py:1420
  202.0 53.2 %finish.1 = (bf16[16384,128]{1,0:T(8,128)(2,1)}, bf16[3328,128]{1,0:T(8,128)(2,1)}) custom-call(bf16[832,128]{1,0:T(8,128)(2,1)} %get-tuple-element.94.refs_0_, bf16[2,2,240,128]{3,2,1,0:T(8,128)(2,1)} %bitcast.31, bf16[1,128,1664]{2,1,0:T(8,128)(2,1)} %get-tuple-element.96.refs_2_, bf16[2,2,16,128]{3,2,1,0:T(8,128)(2,1)} %bitcast.36), custom_call_target="tpu_custom_call" | custom-call | tf_op jit(solution)/shard_map/finish/pallas_call | solution.py:1135
  255.2 8.4 %unpack.1 = (f32[240,2560]{1,0:T(8,128)}, f32[240,2560]{1,0:T(8,128)}, f32[960,640]{1,0:T(8,128)}, f32[240,960]{1,0:T(8,128)}, f32[240,960]{1,0:T(8,128)}, /*ind...) custom-call(bf16[16384,128]{1,0:T(8,128)(2,1)} %get-tuple-element.98.g_in.u_in.d_in.o_in, ...), custom_call_target="tpu_custom_call" | custom-call | tf_op jit(solution)/shard_map/unpack/pallas_call | solution.py:1471

commit v4 on v3

--- a/solution.py
+++ b/solution.py
@@ -75,7 +75,7 @@
         return copy
 
 
-def start_gather(me, sems, local, arrays, stages=None):
+def start_gather(me, sems, local, arrays, stages=None, ringed=None):
     f = me["yl"] * 2 + me["c"]
     near = device(me, yl=1 - me["yl"])
     far = device(me, yl=1 - me["yl"], yh=1 - me["yh"])
@@ -83,6 +83,8 @@
     parts, kept, own = [], [], []
     for i, (a, b) in enumerate(arrays):
         rows = a.shape[0]
+        if i == ringed:
+            continue
         first = rows // 32 * 16 if i % 2 else (rows + 31) // 32 * 16
         for lo, size, dev in ((0, first, near), (first, rows - first, far)):
             if size:
@@ -107,6 +109,51 @@
     return parts, kept, own
 
 
+class Quartered:
+    def __init__(self, me, sems, a, b):
+        self.me, self.sems, self.b = me, sems, b
+        self.rows = a.shape[0]
+        self.quarter = self.rows // 4
+        self.first = (self.quarter + 31) // 32 * 16
+        f = me["yl"] * 2 + me["c"]
+        near = device(me, yl=1 - me["yl"])
+        far = device(me, yl=1 - me["yl"], yh=1 - me["yh"])
+        base = me["x"] * self.quarter
+        self.parts = []
+        for lo, size, dev in ((0, self.first, near), (self.first, self.quarter - self.first, far)):
+            src = a.at[pl.ds(pl.multiple_of(base + lo, 16), size)]
+            dst = b.at[pl.ds(pl.multiple_of(f * self.rows + base + lo, 16), size)]
+            self.parts.append(sems.push(src, dst, dev))
+        self.across = ((1 - me["yl"]) * 2 + me["c"]) * self.rows
+
+    def place(self, at):
+        start = pl.multiple_of(self.across + at * self.quarter, 16)
+        return self.b.at[pl.ds(start, self.quarter)]
+
+    def halves(self, ref):
+        return ref.at[pl.ds(0, self.first)], ref.at[pl.ds(self.first, self.quarter - self.first)]
+
+    def share(self):
+        for copy in self.parts:
+            copy.wait_recv()
+        ring = Ring(self.me, "x")
+        self.shared = Share(self.sems, ring, self.place(ring.me), self.place, self.halves)
+
+    def relay(self):
+        self.shared.relay()
+
+    def pass_on(self):
+        self.shared.arrive()
+        span = self.b.at[pl.ds(pl.multiple_of(self.across, 16), self.rows)]
+        self.mate = self.sems.push(span, span, device(self.me, c=1 - self.me["c"]))
+
+    def end(self):
+        self.shared.end()
+        self.mate.wait()
+        for copy in self.parts:
+            copy.wait_send()
+
+
 def relay_gather(me, sems, started):
     parts, kept, _ = started
     across = (1 - me["yl"]) * 2 + me["c"]
@@ -132,11 +179,10 @@
 
 
 def gather_qkv_kernel(
-    gain_a, gain_b, wq, wk_t, wv_t, gains, qkv, gains_own, qkv_own, send, recv, local
+    both, wq, wk_t, wv_t, gains, qkv, gains_own, qkv_own, send, recv, local
 ):
-    blank = jnp.zeros((1, 16), F32)
-    lines = [jnp.concatenate([g[...].astype(F32), blank], axis=1) for g in (gain_a, gain_b)]
-    gains_own[...] = jnp.concatenate([*lines, jnp.zeros((14, 256), F32)], axis=0).astype(BF16)
+    lines = jnp.concatenate([both[...].astype(F32), jnp.zeros((2, 16), F32)], axis=1)
+    gains_own[...] = jnp.concatenate([lines, jnp.zeros((14, 256), F32)], axis=0).astype(BF16)
     qkv_own[:, 0:896] = wq[:, 0:896]
     rest = [wq[:, 896:960].astype(F32), wk_t[...].astype(F32).T, wv_t[...].astype(F32).T]
     qkv_own[:, 896:1664] = jnp.concatenate([*rest, jnp.zeros((240, 64), F32)], axis=1).astype(BF16)
@@ -149,12 +195,12 @@
     end_gather(started)
 
 
-def gather_qkv(gain_a, gain_b, wq, wk_t, wv_t, collective_id):
+def gather_qkv(both, wq, wk_t, wv_t, collective_id):
     own = [jax.ShapeDtypeStruct((16, 256), BF16), jax.ShapeDtypeStruct((240, 1664), BF16)]
     return pl.pallas_call(
         gather_qkv_kernel,
         out_shape=gathered(own),
-        in_specs=[VM] * 5,
+        in_specs=[VM] * 4,
         out_specs=[ANY] * 2,
         scratch_shapes=[pltpu.VMEM(a.shape, BF16) for a in own]
         + [
@@ -166,7 +212,7 @@
             collective_id=collective_id, has_side_effects=True, vmem_limit_bytes=BIG
         ),
         name="gather_qkv",
-    )(gain_a, gain_b, wq, wk_t, wv_t)
+    )(both, wq, wk_t, wv_t)
 
 
 class Ring:
@@ -242,7 +288,6 @@
         return Share(sems, rings[1 - axis], src, place, halves)
 
     first = [near(axis, yh, kv.at[spans[axis]]) for axis in (0, 1)]
-    once_across()
     out[z, yh, x] = kv[...]
     for share in first:
         share.relay()
@@ -252,6 +297,7 @@
         row = 1 - yh
         src = out.at[z, row, x, spans[axis]]
         second.append(near(axis, row, src))
+    once_across()
     last = []
     for axis in (0, 1):
         first[axis].arrive()
@@ -481,10 +527,12 @@
     me = here()
     greet_axes(me)
     sems = Sems(send, recv)
-    started = []
+    started, quartered = [], []
 
     def start_weights():
-        started.extend(start_gather(me, sems, local, list(zip(shards, full)), stages))
+        quartered.append(Quartered(me, sems, shards[-1], full[-1]))
+        pairs = list(zip(shards, full))
+        started.extend(start_gather(me, sems, local, pairs, stages, count - 1))
 
     across, shares = gather_kv(me, sems, own_ref, kv, start_weights)
     keep = pltpu.make_async_copy(kv, kv_out, local.at[count])
@@ -499,10 +547,16 @@
         l_ref[head] = logs
         return 0
 
-    lax.fori_loop(0, 3, one, 0)
+    down = quartered[0]
+    down.share()
+    lax.fori_loop(0, 1, one, 0)
+    down.relay()
+    lax.fori_loop(1, 3, one, 0)
+    down.pass_on()
     relay_gather(me, sems, started)
     lax.fori_loop(3, KV_HEADS, one, 0)
     end_gather(started)
+    down.end()
     for copy in across:
         copy.wait_send()
     for share in shares:
@@ -513,7 +567,7 @@
 def forward(q, own, plan, shards, collective_id):
     flags, left, _, limits = plan
     n = len(shards)
-    copies = 5 * n + 2 + 8 * 4
+    copies = 5 * n + 3 + 2 + 8 * 4
     return pl.pallas_call(
         functools.partial(forward_kernel, n),
         out_shape=[jax.ShapeDtypeStruct((KV_HEADS, ROWS, 128), F32)] * 2
@@ -1506,7 +1560,7 @@
     w_gate, w_up, w_down,
 ):
     gains, qkv_w = gather_qkv(
-        attn_gain.reshape(1, 240), mlp_gain.reshape(1, 240), w_query, w_key.T, w_value.T, 0
+        jnp.stack([attn_gain, mlp_gain]), w_query, w_key.T, w_value.T, 0
     )
     q_rows, own_kv, na_t, tok, cot, cot_t, cosine, sine, gain_a, gain_b, *plan = project(
         block_table, tokens[0].T, cotangent[0].T, gains, qkv_w

time: 266 us -> 265 us (level)
    pallas_call x1, Pallas kernels: 53.2 us -> 57.4 us  [finish(): pl.pallas_call(functools.partial(finish_kernel, reduction, ready.sizes, r...]
    pallas_call x1, Pallas kernels: 92 us -> 87.9 us  [backward(): pl.pallas_call(functools.partial(backward_kernel, reduction), out_shape=[...]
where the time goes in v4:
time: 265 us; the launch traced here: 264 us
  Pallas kernels  261 us (98%)
    pallas_call x1, Pallas kernels, backward(): pl.pallas_call(functools.partial(backward_kernel, reduction), out_shape=[...  87.9 us
    pallas_call x1, Pallas kernels, forward(): pl.pallas_call(functools.partial(forward_kernel, n), out_shape=[jax.Shape...  63.4 us
    pallas_call x1, Pallas kernels, finish(): pl.pallas_call(functools.partial(finish_kernel, reduction, ready.sizes, r...  57.4 us
    pallas_call x1, Pallas kernels, gather_qkv(): pl.pallas_call(gather_qkv_kernel, out_shape=gathered(own), in_specs=[VM]...  18.3 us
    pallas_call x1, Pallas kernels, middle(): pl.pallas_call(middle_kernel, out_shape=[jax.ShapeDtypeStruct((D, TOK), B...  14.5 us
    pallas_call x1, Pallas kernels, unpack(): pl.pallas_call(unpack_kernel, grid=(5,), out_shape=[jax.ShapeDtypeStruct(...  8.36 us
    pallas_call x1, Pallas kernels, project(): pl.pallas_call(project_kernel, out_shape=[jax.ShapeDtypeStruct((KV_HEADS,...  5.57 us
    pallas_call x1, Pallas kernels, unproject(): pl.pallas_call(unproject_kernel, out_shape=[jax.ShapeDtypeStruct((D, TOK)...  5.46 us

profile of v4, /device:TPU:1, one launch (start us, length us, event | category | flops | bytes accessed | tf_op | source)
XLA Modules:
  0.0 263.7 jit_solution(9936106264051834083)
XLA Ops:
  0.6 0.7 stack.9
  1.3 0.7 stack.10
  2.0 0.6 pad_maximum_fusion.both
  2.5 18.3 %gather_qkv.1 = (bf16[64,256]{1,0:T(8,128)(2,1)}, bf16[960,1664]{1,0:T(8,128)(2,1)}) custom-call(bf16[2,240]{1,0:T(2,128)(2,1)} %pad_maximum_fusion.both, bf16[240,960]{1,0:T(8,128)(2,1)} %wq.1, bf16[320,240]{1,0:T(8,128)(2,1)} %bitcast.34, bf16[320,240]{1,0:T(8,128)(2,1)} %bitcast.35), custom_call_target="tpu_custom_call" | custom-call | tf_op jit(solution)/shard_map/gather_qkv/pallas_call | solution.py:200
  20.9 5.6 %project.1 = (bf16[5,192,128]{2,1,0:T(8,128)(2,1)}, bf16[640,128]{1,0:T(8,128)(2,1)}, bf16[960,128]{1,0:T(8,128)(2,1)}, bf16[128,960]{1,0:T(8,128)(2,1)}, bf16[1...) custom-call(s32[64]{0:T(128)} %table.5, ...), custom_call_target="tpu_custom_call" | custom-call | tf_op jit(solution)/shard_map/project/pallas_call | solution.py:1349
  26.5 63.4 %forward.1 = (f32[5,192,128]{2,1,0:T(8,128)}, f32[5,192,128]{2,1,0:T(8,128)}, bf16[4,2,4,640,128]{4,3,2,1,0:T(8,128)(2,1)}, bf16[960,960]{1,0:T(8,128)(2,1)}, bf...) custom-call(bf16[5,192,128]{2,1,0:T(8,128)(2,1)} %get-tuple-element.62.q_ref.refs_0_, ...), custom_call_target="tpu_custom_call" | custom-call | tf_op jit(solution)/shard_map/forward/pallas_call | solution.py:571
  89.8 14.5 %middle.1 = (bf16[960,128]{1,0:T(8,128)(2,1)}, f32[128,960]{1,0:T(8,128)}, bf16[5,192,128]{2,1,0:T(8,128)(2,1)}, f32[1,960]{1,0:T(1,128)}, bf16[960,128]{1,0:T(8...) custom-call(s32[64]{0:T(128)} %table.5, ...), custom_call_target="tpu_custom_call" | custom-call | tf_op jit(solution)/shard_map/middle/pallas_call | solution.py:1423
  104.3 87.9 %backward.1 = (f32[5,192,128]{2,1,0:T(8,128)}, f32[640,128]{1,0:T(8,128)}, bf16[832,128]{1,0:T(8,128)(2,1)}) custom-call(bf16[5,192,128]{2,1,0:T(8,128)(2,1)} %get-tuple-element.62.q_ref.refs_0_, bf16[5,192,128]{2,1,0:T(8,128)(2,1)} %get-tuple-element.76.refs_1_, f32[5,192,128]{2,1,0:T(8,128)} %get-tuple-element.67.o.refs_2_, ...), custom_call_target="tpu_custom_call" | custom-call | tf_op jit(solution)/shard_map/backward/pallas_call | solution.py:1120
  192.2 5.5 %unproject.1 = (f32[960,128]{1,0:T(8,128)}, bf16[1,128,1664]{2,1,0:T(8,128)(2,1)}, bf16[4,16,128]{2,1,0:T(8,128)(2,1)}) custom-call(s32[64]{0:T(128)} %table.5, f32[5,192,128]{2,1,0:T(8,128)} %get-tuple-element.86.dq, f32[640,128]{1,0:T(8,128)} %get-tuple-element.87.dkv, f32[128,128]{1,0:T(8,128)} %get-tuple-element.88.cosine, ...), custom_call_target="tpu_custom_call" | custom-call | tf_op jit(solution)/shard_map/unproject/pallas_call | solution.py:1474
  197.7 57.4 %finish.1 = (bf16[16384,128]{1,0:T(8,128)(2,1)}, bf16[3328,128]{1,0:T(8,128)(2,1)}) custom-call(bf16[832,128]{1,0:T(8,128)(2,1)} %get-tuple-element.94.refs_0_, bf16[2,2,240,128]{3,2,1,0:T(8,128)(2,1)} %bitcast.31, bf16[1,128,1664]{2,1,0:T(8,128)(2,1)} %get-tuple-element.96.refs_2_, bf16[2,2,16,128]{3,2,1,0:T(8,128)(2,1)} %bitcast.36), custom_call_target="tpu_custom_call" | custom-call | tf_op jit(solution)/shard_map/finish/pallas_call | solution.py:1189
  255.1 8.4 %unpack.1 = (f32[240,2560]{1,0:T(8,128)}, f32[240,2560]{1,0:T(8,128)}, f32[960,640]{1,0:T(8,128)}, f32[240,960]{1,0:T(8,128)}, f32[240,960]{1,0:T(8,128)}, /*ind...) custom-call(bf16[16384,128]{1,0:T(8,128)(2,1)} %get-tuple-element.98.g_in.u_in.d_in.o_in, ...), custom_call_target="tpu_custom_call" | custom-call | tf_op jit(solution)/shard_map/unpack/pallas_call | solution.py:1525
